TPU v7x, 32 devices: a whole 2x2x4 slice. The times are simulated.
32 devices in a mesh: dp: 8 (over z, x), tensor: 4 (over y, core).
Axes of the slice: x: 2, y: 2, z: 4, core: 2. Of those that a mesh axis runs over, the one named last changes fastest.
Arguments:
- images: bfloat16 [40, 197, 768], P('dp'), may hold values from -6 to 6
- w_qkv: bfloat16 [3, 768, 768], P(None, None, 'tensor'), may hold values from -0.21875 to 0.21875
- w_proj: bfloat16 [768, 768], P('tensor'), may hold values from -0.625 to 0.625
- w_router: bfloat16 [768, 4], replicated, may hold values from -0.15625 to 0.15625
- w_in: bfloat16 [4, 768, 3072], P(None, None, 'tensor'), may hold values from -0.21875 to 0.21875
- w_out: bfloat16 [4, 3072, 768], P(None, 'tensor'), may hold values from -0.3125 to 0.3125
- gain_one: float32 [768], replicated, may hold values from 0.5 to 1.5
- gain_two: float32 [768], replicated, may hold values from 0.5 to 1.5
- routes: int32 [40, 197, 2], P('dp'), may hold values from 0 to 3, as said below
- order: int32 [8, 985], P('dp'), may hold values from 0 to 984, each once within a row
- counts: int32 [8], P('dp'), may hold values from 3 to 5, as said below
- cotangent: bfloat16 [40, 197, 768], P('dp'), may hold values from -6 to 6
Outputs:
- output: bfloat16 [40, 197, 768], P('dp')
- grad_images: float32 [40, 197, 768], P('dp')
- grad_qkv: float32 [3, 768, 768], P(None, None, 'tensor')
- grad_proj: float32 [768, 768], P('tensor')
- grad_router: float32 [768, 4], replicated
- grad_in: float32 [4, 768, 3072], P(None, None, 'tensor')
- grad_out: float32 [4, 3072, 768], P(None, 'tensor')
- grad_gain_one: float32 [768], replicated
- grad_gain_two: float32 [768], replicated
- kept: int32 [40, 197, 2], P('dp')
Inputs may be any that keep to these rules, and one draw needn't show every extreme that they name: `routes`: each token names 2 different experts. `order`: each row holds every token position of its group once. `counts`: some group holds all 5 images.
All inputs are finite; a program needn't handle non-finite values.
Results may differ from a plain program's by a relative error of at most 0.024.
Values may be sent and summed in bfloat16 or wider, within the bound.
A program may use at most 192 MiB of HBM per device.

v0:
```python
import jax
import jax.numpy as jnp
from jax import lax
from jax.sharding import PartitionSpec as P

HD = 64
SPECIALIST_TOTAL = 4
TOPK = 2
SEQ = 197
CAP = 616


EPSILON = 1e-06
SCALE = 0.125
HIGHEST = lax.Precision.HIGHEST


def layer_norm(rows, gain):
    center = jnp.mean(rows, axis=-1, keepdims=True)
    centred = rows - center
    spread = jnp.mean(centred * centred, axis=-1, keepdims=True)
    return centred * lax.rsqrt(spread + EPSILON) * gain


def route_slots(routes_g, order_g, count_g):
    tokens = routes_g.shape[0]
    positions = jnp.arange(tokens, dtype=jnp.int32)
    in_image = (positions // SEQ < count_g).astype(jnp.int32)
    capacity_now = (5 * TOPK * count_g * SEQ + 4 * SPECIALIST_TOTAL - 1) // (4 * SPECIALIST_TOTAL)
    ranked = routes_g[order_g]
    alive_rows = in_image[order_g]
    pair_expert = ranked.T.reshape(-1)
    pair_alive = jnp.tile(alive_rows, TOPK)
    matches = (
        pair_expert[:, None] == jnp.arange(SPECIALIST_TOTAL, dtype=jnp.int32)[None, :]
    ).astype(jnp.int32) * pair_alive[:, None]
    before = jnp.cumsum(matches, axis=0) - matches
    pair_slot = jnp.sum(before * matches, axis=1)
    pair_kept = pair_alive * (pair_slot < capacity_now).astype(jnp.int32)
    inverse = jnp.zeros((tokens,), jnp.int32).at[order_g].set(positions)
    slot_of = pair_slot.reshape(TOPK, tokens)[:, inverse].T
    kept_pairs = pair_kept.reshape(TOPK, tokens)[:, inverse].T
    return (slot_of, kept_pairs)


def reduce_experts(grad_w_in, grad_w_out):
    share_in, share_out = (
        lax.psum_scatter(grad_w_in, "dp", scatter_dimension=1, tiled=True),
        lax.psum_scatter(grad_w_out, "dp", scatter_dimension=2, tiled=True),
    )
    return (
        lax.all_gather(share_in.astype(jnp.bfloat16), "dp", axis=1, tiled=True).astype(
            share_in.dtype
        ),
        lax.all_gather(share_out.astype(jnp.bfloat16), "dp", axis=2, tiled=True).astype(
            share_out.dtype
        ),
    )


def per_device(
    images,
    w_qkv,
    w_proj,
    w_router,
    w_in,
    w_out,
    gain_one,
    gain_two,
    routes,
    order,
    counts,
    cotangent,
):
    img_count, seq_len, width = images.shape
    tokens = img_count * seq_len
    local = w_proj.shape[0]
    heads = local // HD
    rows = images.reshape(tokens, width).astype(jnp.float32)
    routes_g = routes.reshape(tokens, TOPK)
    slot_of, kept_pairs = route_slots(routes_g, order[0], counts[0])
    normed = layer_norm(rows, gain_one).astype(jnp.bfloat16)
    projected = jnp.einsum("td,sdc->stc", normed, w_qkv, preferred_element_type=jnp.float32).astype(
        jnp.bfloat16
    )
    shaped = projected.reshape(3, img_count, seq_len, heads, HD)
    queries, keys, values = (shaped[0], shaped[1], shaped[2])
    precedence_measures = (
        jnp.einsum("inhc,imhc->ihnm", queries, keys, preferred_element_type=jnp.float32) * SCALE
    )
    peak = jnp.max(precedence_measures, axis=-1, keepdims=True)
    log_total = peak + jnp.log(jnp.sum(jnp.exp(precedence_measures - peak), axis=-1, keepdims=True))
    probs = jnp.exp(precedence_measures - log_total).astype(jnp.bfloat16)
    mixed = jnp.einsum("ihnm,imhc->inhc", probs, values, preferred_element_type=jnp.float32)
    mixed = mixed.astype(jnp.bfloat16).reshape(tokens, local)
    partial_attn = jnp.dot(mixed, w_proj, preferred_element_type=jnp.float32)
    hidden_one = rows + lax.psum(partial_attn.astype(jnp.bfloat16), "tensor").astype(jnp.float32)
    normed_two = layer_norm(hidden_one, gain_two).astype(jnp.bfloat16)
    logits = jnp.dot(normed_two, w_router, preferred_element_type=jnp.float32)
    gates_all = jax.nn.softmax(logits, axis=-1)
    choose = (routes_g[:, :, None] == jnp.arange(SPECIALIST_TOTAL, dtype=jnp.int32)).astype(
        jnp.float32
    )
    chosen = jnp.sum(choose * gates_all[:, None, :], axis=-1)
    flat_slot = (routes_g * CAP + slot_of).T
    columns = jnp.arange(SPECIALIST_TOTAL * CAP, dtype=jnp.int32)
    select = ((flat_slot[:, :, None] == columns) & (kept_pairs.T[:, :, None] > 0)).astype(
        jnp.bfloat16
    )
    slots_in = jnp.einsum("kte,td->ed", select, normed_two, preferred_element_type=jnp.float32)
    slots_in = slots_in.astype(jnp.bfloat16).reshape(SPECIALIST_TOTAL, CAP, width)
    inner = jnp.einsum("ecd,edf->ecf", slots_in, w_in, preferred_element_type=jnp.float32)
    active = jax.nn.gelu(inner).astype(jnp.bfloat16)
    expert_rows = jnp.einsum("ecf,efd->ecd", active, w_out, preferred_element_type=jnp.float32)
    expert_rows = expert_rows.astype(jnp.bfloat16).reshape(SPECIALIST_TOTAL * CAP, width)
    picked = jnp.einsum("kte,ed->ktd", select, expert_rows, preferred_element_type=jnp.float32)
    gate_weights = chosen.T * kept_pairs.T.astype(jnp.float32)
    partial_moe = jnp.sum(picked * gate_weights[:, :, None], axis=0)
    output = hidden_one + lax.psum(partial_moe.astype(jnp.bfloat16), "tensor").astype(jnp.float32)
    back = cotangent.reshape(tokens, width).astype(jnp.float32)
    gate_part = kept_pairs.T.astype(jnp.float32) * jnp.sum(picked * back[None], axis=-1)
    scaled_back = (gate_weights[:, :, None] * back[None]).astype(jnp.bfloat16)
    grad_rows_out = jnp.einsum(
        "kte,ktd->ed", select, scaled_back, preferred_element_type=jnp.float32
    )
    grad_rows_out = grad_rows_out.astype(jnp.bfloat16).reshape(SPECIALIST_TOTAL, CAP, width)
    grad_w_out = jnp.einsum(
        "ecf,ecd->efd", active, grad_rows_out, preferred_element_type=jnp.float32
    )
    grad_active = jnp.einsum(
        "ecd,efd->ecf", grad_rows_out, w_out, preferred_element_type=jnp.float32
    )
    _, gelu_back = jax.vjp(jax.nn.gelu, inner)
    grad_inner = gelu_back(grad_active)[0].astype(jnp.bfloat16)
    grad_w_in = jnp.einsum("ecd,ecf->edf", slots_in, grad_inner, preferred_element_type=jnp.float32)
    grad_slots = jnp.einsum("ecf,edf->ecd", grad_inner, w_in, preferred_element_type=jnp.float32)
    grad_slots = grad_slots.astype(jnp.bfloat16).reshape(SPECIALIST_TOTAL * CAP, width)
    part_normed = jnp.einsum("kte,ed->td", select, grad_slots, preferred_element_type=jnp.float32)
    sum_normed, sum_gates = (
        lax.psum(part_normed.astype(jnp.bfloat16), "tensor").astype(jnp.float32),
        lax.psum(gate_part.astype(jnp.bfloat16), "tensor").astype(jnp.float32),
    )
    grad_gates = jnp.sum(choose * sum_gates.T[:, :, None], axis=1)
    grad_logits = gates_all * (grad_gates - jnp.sum(gates_all * grad_gates, axis=-1, keepdims=True))
    grad_router = jnp.dot(normed_two.astype(jnp.float32).T, grad_logits, precision=HIGHEST)
    deriv_standardized_second = sum_normed + jnp.dot(
        grad_logits, w_router.astype(jnp.float32).T, precision=HIGHEST
    )
    _, norm_back_two = jax.vjp(layer_norm, hidden_one, gain_two)
    grad_hidden_part, grad_gain_two = norm_back_two(deriv_standardized_second)
    grad_hidden = back + grad_hidden_part
    grad_attn = grad_hidden.astype(jnp.bfloat16)
    grad_proj = jnp.einsum("tc,td->cd", mixed, grad_attn, preferred_element_type=jnp.float32)
    grad_mixed = jnp.einsum("td,cd->tc", grad_attn, w_proj, preferred_element_type=jnp.float32)
    grad_mixed = grad_mixed.astype(jnp.bfloat16).reshape(img_count, seq_len, heads, HD)
    again = jnp.einsum("inhc,imhc->ihnm", queries, keys, preferred_element_type=jnp.float32) * SCALE
    probs_again = jnp.exp(again - log_total)
    grad_values = jnp.einsum(
        "ihnm,inhc->imhc",
        probs_again.astype(jnp.bfloat16),
        grad_mixed,
        preferred_element_type=jnp.float32,
    )
    grad_probs = jnp.einsum(
        "inhc,imhc->ihnm", grad_mixed, values, preferred_element_type=jnp.float32
    )
    centre_term = jnp.sum(probs_again * grad_probs, axis=-1, keepdims=True)
    grad_scores = (probs_again * (grad_probs - centre_term)).astype(jnp.bfloat16)
    query_gradient = (
        jnp.einsum("ihnm,imhc->inhc", grad_scores, keys, preferred_element_type=jnp.float32) * SCALE
    )
    grad_keys = (
        jnp.einsum("ihnm,inhc->imhc", grad_scores, queries, preferred_element_type=jnp.float32)
        * SCALE
    )
    grad_projected = (
        jnp.stack([query_gradient, grad_keys, grad_values])
        .astype(jnp.bfloat16)
        .reshape(3, tokens, local)
    )
    grad_qkv = jnp.einsum("td,stc->sdc", normed, grad_projected, preferred_element_type=jnp.float32)
    part_normed_one = jnp.einsum(
        "stc,sdc->td", grad_projected, w_qkv, preferred_element_type=jnp.float32
    )
    sum_normed_one = lax.psum(part_normed_one.astype(jnp.bfloat16), "tensor").astype(jnp.float32)
    _, norm_back_one = jax.vjp(layer_norm, rows, gain_one)
    partial_row_gradient, grad_gain_one = norm_back_one(sum_normed_one)
    grad_input = grad_hidden + partial_row_gradient
    dense = lax.psum((grad_qkv, grad_proj, grad_router, grad_gain_one, grad_gain_two), "dp")
    summed_in, summed_out = reduce_experts(grad_w_in, grad_w_out)
    return (
        output.astype(jnp.bfloat16).reshape(images.shape),
        grad_input.reshape(images.shape),
        dense[0],
        dense[1],
        dense[2],
        summed_in,
        summed_out,
        dense[3],
        dense[4],
        kept_pairs.reshape(img_count, seq_len, TOPK),
    )


def solution(mesh):
    return jax.shard_map(
        per_device,
        mesh=mesh,
        in_specs=(
            P("dp", None, None),
            P(None, None, "tensor"),
            P("tensor", None),
            P(),
            P(None, None, "tensor"),
            P(None, "tensor", None),
            P(),
            P(),
            P("dp", None, None),
            P("dp", None),
            P("dp"),
            P("dp", None, None),
        ),
        out_specs=(
            P("dp", None, None),
            P("dp", None, None),
            P(None, None, "tensor"),
            P("tensor", None),
            P(),
            P(None, None, "tensor"),
            P(None, "tensor", None),
            P(),
            P(),
            P("dp", None, None),
        ),
        check_vma=False,
    )
```

profile of v0, /device:TPU:0, one launch (start us, length us, event | category | flops | bytes accessed | tf_op | source)
XLA Modules:
  0.0 848.9 jit_solution(9710391304719548678)
XLA Ops:
  7.3 3.5 reshape.234
  11.9 3.1 fusion.66
  15.3 1.7 squeeze.15
  17.0 0.8 squeeze.17
  17.8 0.8 squeeze.16
  18.5 0.7 multiply_reduce_fusion.7
  19.9 0.7 fusion.29
  21.2 0.6 reshape.221
  21.8 1.8 convolution_convert_fusion.4
  24.5 5.4 scatter_custom_fusion
  30.0 4.5 gather_fusion.1
  34.8 2.9 gather_fusion
  38.0 1.2 reduce-window.6
  40.1 1.0 compare_select_fusion
  41.1 3.9 gather_fusion.3
  45.3 2.9 gather_fusion.2
  48.2 3.4 reshape.235
  52.0 7.7 convert_reduce_fusion
  59.7 9.0 %all-reduce.9.cloned.1.call-done = bf16[985,768]{1,0:T(8,128)(2,1)} async-done(((bf16[985,768]{1,0:T(8,128)(2,1)}), bf16[985,768]{1,0:T(8,128)(2,1)}) %all-reduce.9.cloned.1.call-update) | async-done | bytes 1512976 | tf_op jit(solution)/shard_map/psum | solution.py:97
  68.7 2.8 fusion.69
  73.8 5.5 fusion.74
  79.4 10.9 %bitcast_convert_fusion = bf16[2464,768]{1,0:T(8,128)(2,1)S(1)} fusion(s32[2,985]{1,0:T(2,128)S(1)} %add_bitcast_fusion.1, pred[2,985]{1,0:T(4,128)(4,1)S(1)} %copy.148, f32[985,768]{1,0:T(8,128)S(1)} %copy-done.13, f32[2,985]{1,0:T(2,128)S(1)} %bitcast_multiply_fusion.1), kind=kOutput, calls=%fused_computation.24 | convolution fusion | flops 7470493184 | bytes 6828354 | tf_op jit(solution)/shard_map/kte,ktd->ed/dot_general | solution.py:123
  90.4 5.3 fusion.72
  95.7 12.0 %fusion.16 = (bf16[4,616,768]{2,1,0:T(8,128)(2,1)S(1)}, f32[4,616,768]{2,1,0:T(8,128)}) fusion(f32[4,616,768]{2,1,0:T(8,128)} %fusion.72, bf16[4,616,768]{2,1,0:T(8,128)(2,1)} %bitcast.130, bf16[4,768,768]{2,1,0:T(8,128)(2,1)S(1)} %bitcast.125), kind=kOutput, calls=%fused_computation.23 | convolution fusion | flops 2944499712 | bytes 27426816 | tf_op jit(solution)/shard_map/ecd,edf->ecf/dot_general | solution.py:112
  107.7 3.8 convolution_convert_fusion.1
  111.5 5.5 fusion.75
  117.1 10.9 %fusion.73 = f32[4,768,768]{2,1,0:T(8,128)} fusion(bf16[4,616,768]{2,1,0:T(8,128)(2,1)} %bitcast.131, bf16[4,616,768]{2,1,0:T(8,128)(2,1)} %copy-done.39), kind=kOutput, calls=%fused_computation.154 | convolution fusion | flops 2906652672 | bytes 17006592 | tf_op jit(solution)/shard_map/ecd,ecf->edf/dot_general | solution.py:135
  128.1 12.4 %fusion.67 = f32[4,768,768]{1,2,0:T(8,128)} fusion(bf16[4,616,768]{2,1,0:T(8,128)(2,1)} %bitcast.129, f32[4,616,768]{2,1,0:T(8,128)} %get-tuple-element.85), kind=kOutput, calls=%fused_computation.148 | convolution fusion | flops 2923683840 | bytes 20791296 | tf_op jit(solution)/shard_map/ecf,ecd->efd/dot_general | solution.py:127
  140.7 8.4 convolution_convert_fusion.2
  149.1 11.7 %multiply_reduce_fusion = (f32[2,985]{1,0:T(2,128)S(1)}, bf16[985,768]{1,0:T(8,128)(2,1)}) fusion(f32[985,768]{1,0:T(8,128)S(1)} %copy-done.14, f32[2,985]{1,0:T(2,128)S(1)} %bitcast_multiply_fusion.1, bf16[2464,768,1]{1,0,2:T(8,128)(2,1)S(1)} %bitcast.132, s32[2,985]{1,0:T(2,128)S(1)} %add_bitcast_fusion.1, pred[2,985]{1,0:T(4,128)(4,1)S(1)} %copy.148), kind=kOutput, calls=%fused_computation.26 | convolution fusion | flops 7470868480 | bytes 8349194 | tf_op jit(solution)/shard_map/kte,ed->ktd/dot_general | solution.py:116
  160.9 6.0 psum.73
  167.0 5.2 multiply_reduce_fusion.4
  172.2 1.5 fusion.68
  174.5 1.6 copy-done.7
  176.0 0.6 convolution_convert_fusion.7
  176.7 1.6 reshape.231
  178.3 3.4 multiply_reduce_fusion.2
  181.7 0.9 multiply_convert_fusion.2
  183.3 1.2 copy.154
  184.5 2.5 stack.12
  188.5 2.9 fusion.30
  192.4 2.5 bitcast_convert_fusion.1
  195.3 131.8 %reduce-scatter.3.cloned.1.call-done = f32[4,96,768]{2,1,0:T(8,128)} async-done(((f32[4,768,768]{2,1,0:T(8,128)}), f32[4,96,768]{2,1,0:T(8,128)}) %reduce-scatter.3.cloned.1.call-update) | async-done | bytes 1179664 | tf_op jit(solution)/shard_map/reduce_scatter | solution.py:48
  327.1 2.2 convert_element_type.172
  329.4 164.3 %reduce-scatter.5.cloned.1.call-done = f32[4,768,96]{1,2,0:T(8,128)} async-done(((f32[4,768,768]{1,2,0:T(8,128)}), f32[4,768,96]{1,2,0:T(8,128)}) %reduce-scatter.5.cloned.1.call-update) | async-done | bytes 1179664 | tf_op jit(solution)/shard_map/reduce_scatter | solution.py:49
  493.7 2.1 convert_element_type.174
  496.0 3.3 fusion.33
  499.3 3.9 convolution_bitcast_fusion
  504.0 0.7 fusion.60
  504.7 58.0 %all-reduce.15.cloned.1.call-done = (bf16[985,768]{1,0:T(8,128)(2,1)}, bf16[985,768]{1,0:T(8,128)(2,1)}) async-done(((bf16[985,768]{1,0:T(8,128)(2,1)}, bf16[985,768]{1,0:T(8,128)(2,1)}), (bf16[985,768]{1,0:T(8,128)(2,1)}, bf16[985,768]{1,0:T(8,128)(2,1)})) %all-reduce.15.cloned.1.call-update) | async-done | bytes 3025936 | tf_op jit(solution)/shard_map/psum | solution.py:119
  562.7 3.9 add_convert_fusion
  566.6 3.0 reshape.228
  569.5 2.7 fusion.21
  572.4 1.9 fusion.22
  574.4 2.4 add_add_fusion.2
  576.7 3.9 reshape.232
  580.6 38.8 %all-reduce.1 = (f32[768,4]{0,1:T(4,128)}, f32[768]{0:T(1024)}, f32[768]{0:T(1024)}) all-reduce(f32[768,4]{0,1:T(4,128)S(1)} %fusion.60, f32[768]{0:T(1024)S(1)} %get-tuple-element.64, f32[768]{0:T(1024)S(1)} %get-tuple-element.60), channel_id=1, replica_groups=mesh['dp'=8,'tensor'=4] {'dp'}, use_global_device_ids=true, to_apply=%region_30.31 | all-reduce | flops 4608 | bytes 36864 | tf_op jit(solution)/shard_map/psum | solution.py:189
  619.3 26.3 %all-gather.3.cloned.1.call-done = bf16[4,768,768]{2,1,0:T(8,128)(2,1)} async-done(((bf16[4,96,768]{2,1,0:T(8,128)(2,1)}), bf16[4,768,768]{2,1,0:T(8,128)(2,1)}) %all-gather.3.cloned.1.call-update) | async-done | bytes 4718608 | tf_op jit(solution)/shard_map/all_gather | solution.py:52
  645.6 6.9 convert_element_type.173
  652.5 73.6 %all-gather.5.cloned.1.call-done = bf16[4,768,768]{1,2,0:T(8,128)(2,1)} async-done(((bf16[4,768,96]{1,2,0:T(8,128)(2,1)}), bf16[4,768,768]{1,2,0:T(8,128)(2,1)}) %all-gather.5.cloned.1.call-update) | async-done | bytes 4718608 | tf_op jit(solution)/shard_map/all_gather | solution.py:55
  726.1 7.4 copy.162
  733.5 104.4 %all-reduce.13.cloned.1.call-done = (f32[3,768,192]{1,2,0:T(8,128)}, f32[192,768]{1,0:T(8,128)}) async-done(((f32[3,768,192]{1,2,0:T(8,128)}, f32[192,768]{1,0:T(8,128)}), (f32[3,768,192]{1,2,0:T(8,128)}, f32[192,768]{1,0:T(8,128)})) %all-reduce.13.cloned.1.call-update) | async-done | bytes 2359312 | tf_op jit(solution)/shard_map/psum | solution.py:189
  837.9 2.9 copy.207
  840.8 0.8 copy.208
  (179 shorter events, 12.8 us)
Async XLA Ops:
  7.2 4.7 copy-start
  7.2 3.6 copy-start.9
  7.2 4.7 copy-start.30
  7.2 61.5 %all-reduce.9.cloned.1.call-start = ((), (), s32[]{:S(2)}) async-start(), calls=%async_computation.2 | async-start | bytes 3047424 | tf_op jit(solution)/shard_map/psum | solution.py:97
  11.7 3.3 copy-start.26
  11.8 3.2 copy-start.32
  11.8 3.2 copy-start.28
  17.7 2.1 copy-start.16
  18.5 1.3 copy-start.18
  19.2 1.6 copy-start.1
  19.9 1.9 copy-start.23
  20.9 3.4 copy-start.36
  20.9 3.6 copy-start.37
  21.8 2.6 copy-start.20
  23.6 143.3 %all-reduce.11.cloned.1.call-start = ((), (), s32[]{:S(2)}) async-start(), calls=%async_computation.3 | async-start | bytes 3047424 | tf_op jit(solution)/shard_map/psum | solution.py:140
  68.7 5.1 slice-start
  71.5 1.6 copy-start.3
  71.5 0.7 copy-start.34
  71.6 1.6 copy-start.35
  71.6 2.2 slice-start.1
  73.1 6.2 copy-start.10
  73.8 5.6 copy-start.13
  73.8 16.6 %slice-start.4 = ((s8[4718592]{0:T(1024)(128)(4,1)}), s8[4194304]{0:T(1024)(128)(4,1)S(1)}, s32[]{:S(2)}) async-start(s8[4718592]{0:T(1024)(128)(4,1)} %bitcast.126), calls=%async_computation.14 | async-start | bytes 8388608
  73.8 21.9 %slice-start.2 = ((s8[4718592]{0:T(1024)(128)(4,1)}), s8[4194304]{0:T(1024)(128)(4,1)S(1)}, s32[]{:S(2)}) async-start(s8[4718592]{0:T(1024)(128)(4,1)} %bitcast.124), calls=%async_computation.12 | async-start | bytes 8388608
  79.4 11.0 %slice-start.5 = ((s8[4718592]{0:T(1024)(128)(4,1)}), s8[524288]{0:T(1024)(128)(4,1)S(1)}, s32[]{:S(2)}) async-start(s8[4718592]{0:T(1024)(128)(4,1)} %bitcast.126), calls=%async_computation.15 | async-start | bytes 1048576
  79.4 16.3 %slice-start.3 = ((s8[4718592]{0:T(1024)(128)(4,1)}), s8[524288]{0:T(1024)(128)(4,1)S(1)}, s32[]{:S(2)}) async-start(s8[4718592]{0:T(1024)(128)(4,1)} %bitcast.124), calls=%async_computation.13 | async-start | bytes 1048576
  90.4 5.3 copy-start.38
  107.7 3.8 copy-start.39
  117.1 210.0 %reduce-scatter.3.cloned.1.call-start = ((), (), s32[]{:S(2)}) async-start(), calls=%async_computation.4 | async-start | bytes 10616832 | tf_op jit(solution)/shard_map/reduce_scatter | solution.py:48
  128.0 365.7 %reduce-scatter.5.cloned.1.call-start = ((), (), s32[]{:S(2)}) async-start(), calls=%async_computation.6 | async-start | bytes 10616832 | tf_op jit(solution)/shard_map/reduce_scatter | solution.py:49
  140.5 422.2 %all-reduce.15.cloned.1.call-start = ((), (), s32[]{:S(2)}) async-start(), calls=%async_computation.9 | async-start | bytes 6094848 | tf_op jit(solution)/shard_map/psum | solution.py:119
  140.7 8.4 copy-start.14
  166.9 5.3 copy-start.4
  172.2 1.9 copy-start.15
  174.4 1.6 copy-start.7
  176.0 2.3 copy-start.19
  178.3 3.4 copy-start.2
  181.7 1.1 copy-start.17
  188.5 3.8 copy-start.22
  192.4 2.5 copy-start.25
  195.0 301.0 %copy-start.21 = (bf16[985,192]{0,1:T(8,128)(2,1)S(1)}, bf16[985,192]{0,1:T(8,128)(2,1)}, u32[]{:S(2)}) copy-start(bf16[985,192]{0,1:T(8,128)(2,1)} %copy-done.20) | copy-start | bytes 1134724
  195.0 450.6 %all-gather.3.cloned.1.call-start = ((), (), s32[]{:S(2)}) async-start(), calls=%async_computation.5 | async-start | bytes 5308416 | tf_op jit(solution)/shard_map/all_gather | solution.py:52
  329.4 169.9 %copy-start.27 = (f32[985]{0:T(1024)S(1)}, f32[985]{0:T(1024)}, u32[]{:S(2)}) copy-start(f32[985]{0:T(1024)} %copy-done.26) | copy-start | bytes 11824
  329.4 169.9 %copy-start.29 = (f32[985]{0:T(1024)S(1)}, f32[985]{0:T(1024)}, u32[]{:S(2)}) copy-start(f32[985]{0:T(1024)} %copy-done.28) | copy-start | bytes 11824
  329.4 169.9 %copy-start.31 = (f32[768]{0:T(1024)S(1)}, f32[768]{0:T(1024)}, u32[]{:S(2)}) copy-start(f32[768]{0:T(1024)} %param.18) | copy-start | bytes 9220
  329.4 396.7 %all-gather.5.cloned.1.call-start = ((), (), s32[]{:S(2)}) async-start(), calls=%async_computation.7 | async-start | bytes 5308416 | tf_op jit(solution)/shard_map/all_gather | solution.py:55
  495.9 342.1 %all-reduce.13.cloned.1.call-start = ((), (), s32[]{:S(2)}) async-start(), calls=%async_computation.8 | async-start | bytes 4718592 | tf_op jit(solution)/shard_map/psum | solution.py:189
  496.0 3.3 copy-start.5
  499.3 4.7 copy-start.11
  562.7 6.8 copy-start.12
  566.6 5.7 copy-start.33
  569.5 2.8 copy-start.6
  572.3 2.1 copy-start.8
  837.9 2.9 copy-start.24
Sparse Core Ops, SparseCore 0:
  23.7 44.9 all-reduce.8
  117.2 42.2 all-reduce.10
  163.7 163.4 reduce-scatter.2
  331.1 162.5 reduce-scatter.4
  496.5 66.1 all-reduce.14
  565.0 80.5 all-gather.2
  648.0 78.0 all-gather.4
  730.7 107.2 all-reduce.12
where the time goes:
time: 856 us; the launch traced here: 849 us
  waiting for transfers between devices  568 us (66%)
  matrix products  117 us (14%)
  local copies, waits for them, and re-layouts  62 us (7%)
  blocking collectives  44.7 us (5%)
  other arithmetic  40.8 us (5%)
  between operations  16.3 us (2%)
    reduce_scatter x1, waiting for transfers between devices, reduce_experts(): lax.psum_scatter(grad_w_out, 'dp', scatter_dimension=2, tiled=True)  164 us
    reduce_scatter x1, waiting for transfers between devices, reduce_experts(): lax.psum_scatter(grad_w_in, 'dp', scatter_dimension=1, tiled=True)  132 us
    psum x1, waiting for transfers between devices, per_device(): lax.psum((grad_qkv, grad_proj, grad_router, grad_gain_one, grad_gain_two)...  104 us
    all_gather x1, waiting for transfers between devices, reduce_experts(): lax.all_gather(share_out.astype(jnp.bfloat16), 'dp', axis=2, tiled=True)  73.6 us
    psum x1, waiting for transfers between devices, per_device(): lax.psum(partial_moe.astype(jnp.bfloat16), 'tensor').astype(jnp.float32)  58 us
    psum x1, blocking collectives, per_device(): lax.psum((grad_qkv, grad_proj, grad_router, grad_gain_one, grad_gain_two)...  38.8 us
    all_gather x1, waiting for transfers between devices, reduce_experts(): lax.all_gather(share_in.astype(jnp.bfloat16), 'dp', axis=1, tiled=True)  26.3 us
  transfers between devices with their start and end apart: 8, of which 7 were waited for; matrix products, arithmetic and copies ran while one was open for 18% of the time, Pallas kernels for 0%

commit v1 on v0

v1 whole, which is shorter than its diff:
```python
import functools

import jax
import jax.numpy as jnp
from jax import lax
from jax.experimental import pallas as pl
from jax.experimental.pallas import tpu as pltpu
from jax.sharding import PartitionSpec as P

HD = 64
SPECIALIST_TOTAL = 4
TOPK = 2
SEQ = 197
SEQ_PAD = 208
CAP = 616
CAP_PAD = 640
TILE = 320
PAIRED = SPECIALIST_TOTAL // 2
LANES = 128
PIECE = 128
RING = 4
DENSE_CUTS = ((0, 96), (96, 96), (192, 96), (288, 96), (384, 16))
DENSE_HALF = 400


EPSILON = 1e-06
SCALE = 0.125
BF = jnp.bfloat16
F32 = jnp.float32
MESH = pl.DeviceIdType.MESH
VMEM_LIMIT = 62 * 2**20


def dot(left, right, left_dim=1, right_dim=0):
    return lax.dot_general(
        left, right, (((left_dim,), (right_dim,)), ((), ())), preferred_element_type=F32
    )


def lane_ids(shape):
    return lax.broadcasted_iota(jnp.int32, shape, len(shape) - 1)


def standardize(rows):
    center = jnp.mean(rows, axis=-1, keepdims=True)
    centred = rows - center
    spread = jnp.mean(centred * centred, axis=-1, keepdims=True)
    root = lax.rsqrt(spread + EPSILON)
    return centred * root, root


def norm_back(grad, plain, root, gain):
    grad = grad * gain
    first = jnp.mean(grad, axis=-1, keepdims=True)
    second = jnp.mean(grad * plain, axis=-1, keepdims=True)
    return root * (grad - first - plain * second)


def route_slots(routes_g, order_g, count_g):
    tokens = routes_g.shape[0]
    positions = jnp.arange(tokens, dtype=jnp.int32)
    in_image = (positions // SEQ < count_g).astype(jnp.int32)
    capacity_now = (5 * TOPK * count_g * SEQ + 4 * SPECIALIST_TOTAL - 1) // (4 * SPECIALIST_TOTAL)
    spots = order_g[:, None] == positions[None, :]
    place = jnp.sum(jnp.where(spots, positions[:, None], 0), axis=0)
    earlier = (place[None, :] < place[:, None]).astype(BF)
    experts = jnp.arange(SPECIALIST_TOTAL, dtype=jnp.int32)
    marks = (routes_g[:, :, None] == experts).astype(jnp.int32) * in_image[:, None, None]
    marks = marks.reshape(tokens, TOPK * SPECIALIST_TOTAL)
    before = jnp.dot(earlier, marks.astype(BF), preferred_element_type=F32)
    before = before.reshape(tokens, TOPK, SPECIALIST_TOTAL).astype(jnp.int32)
    marks = marks.reshape(tokens, TOPK, SPECIALIST_TOTAL)
    first_total = jnp.sum(marks[:, 0, :], axis=0)
    before = before + jnp.stack([jnp.zeros_like(first_total), first_total])[None]
    slot_of = jnp.sum(before * marks, axis=-1)
    kept_pairs = in_image[:, None] * (slot_of < capacity_now).astype(jnp.int32)
    held = jnp.max(jnp.where((marks * kept_pairs[:, :, None]) > 0, before, -1), axis=1)
    return (held, kept_pairs)


def pair_sum(partial):
    n_t = lax.axis_size("tensor")
    core = lax.axis_index("tensor") % 2
    half = partial.shape[-1] // 2
    other = [(i, i ^ 1) for i in range(n_t)]
    mine = lax.dynamic_slice_in_dim(partial, core * half, half, partial.ndim - 1)
    gone = lax.dynamic_slice_in_dim(partial, (1 - core) * half, half, partial.ndim - 1)
    got = lax.ppermute(gone, "tensor", other)
    total = (mine.astype(F32) + got.astype(F32)).astype(BF)
    step = 2
    while step < n_t:
        got = lax.ppermute(total, "tensor", [(i, i ^ step) for i in range(n_t)])
        total = (total.astype(F32) + got.astype(F32)).astype(BF)
        step *= 2
    back = lax.ppermute(total, "tensor", other)
    return jnp.where(
        core == 0,
        jnp.concatenate([total, back], axis=-1),
        jnp.concatenate([back, total], axis=-1),
    )


def head_mask(shape, head):
    return lane_ids(shape) // HD == head


def image_rows(i):
    return pl.ds(pl.multiple_of(i * SEQ_PAD, 16), SEQ_PAD)


def attend(query, key, head):
    alone = jnp.where(head_mask(query.shape, head), query, jnp.zeros_like(query))
    scores = dot(alone, key, 1, 1) * SCALE
    scores = jnp.where(lane_ids(scores.shape) < SEQ, scores, -jnp.inf)
    powers = jnp.exp(scores - jnp.max(scores, axis=-1, keepdims=True))
    return powers / jnp.sum(powers, axis=-1, keepdims=True)


def attention_image(i, images, w_qkv, w_proj, gain, partial, qkv, mixed):
    at = image_rows(i)
    plain, _ = standardize(images[at, :].astype(F32))
    normed = (plain * gain[...]).astype(BF)
    for s in range(3):
        qkv[s, at, :] = dot(normed, w_qkv[s]).astype(BF)
    query, key, value = (qkv[s, at, :] for s in range(3))
    result = jnp.zeros(query.shape, F32)
    for head in range(query.shape[1] // HD):
        weights = attend(query, key, head).astype(BF)
        result = jnp.where(head_mask(query.shape, head), dot(weights, value), result)
    result = result.astype(BF)
    mixed[at, :] = result
    partial[at, :] = dot(result, w_proj[...]).astype(BF)


def softmax_of(logits, axis):
    ids = lax.broadcasted_iota(jnp.int32, logits.shape, axis)
    logits = jnp.where(ids < SPECIALIST_TOTAL, logits, -jnp.inf)
    powers = jnp.exp(logits - jnp.max(logits, axis=axis, keepdims=True))
    return powers / jnp.sum(powers, axis=axis, keepdims=True)


def second_norm_image(i, images, attended, gain, normed):
    at = image_rows(i)
    plain, _ = standardize(images[at, :].astype(F32) + attended[at, :].astype(F32))
    normed[at, :] = (plain * gain[...]).astype(BF)


def gelu_both(rows):
    inner = 0.7978845608028654 * (rows + 0.044715 * rows * rows * rows)
    curve = jnp.tanh(inner)
    half = 0.5 * (1.0 + curve)
    slope = half + 0.5 * rows * (1.0 - curve * curve) * (
        0.7978845608028654 * (1.0 + 3.0 * 0.044715 * rows * rows)
    )
    return rows * half, slope


def expert_rows(expert, tokens, back, held, gates, w_in, w_out, factors, offset, sent, tick):
    width = tokens.shape[1]
    row = held[pl.ds(expert, 1), :]
    gate = gates[pl.ds(expert, 1), :]

    def tile(i, carry):
        ids = lax.broadcasted_iota(jnp.int32, (TILE, row.shape[1]), 0) + i * TILE
        hit = ids == row
        pick = jnp.where(hit, 1.0, 0.0).astype(BF)
        scale = jnp.sum(jnp.where(hit, gate, 0.0), axis=1, keepdims=True)
        buffer = dot(pick, tokens[...]).astype(BF)
        raw = dot(pick, back[...])
        grad = (scale * raw).astype(BF)
        value, slope = gelu_both(dot(buffer, w_in[...]))
        value = value.astype(BF)
        delta = (dot(grad, w_out[...], 1, 1) * slope).astype(BF)
        if factors is not None:
            at = pl.ds(pl.multiple_of(offset + i * TILE, 16), TILE)
            for ref, rows in zip(factors, (buffer, delta, value, grad)):
                ref[at, :] = rows
        if sent is not None:
            at = pl.ds(pl.multiple_of(i * TILE, 16), TILE)
            out = dot(value, w_out[...]).astype(BF).astype(F32)
            share = jnp.sum(out * raw, axis=1, keepdims=True)
            sent[at, :width] = (scale * out).astype(BF)
            sent[at, width : 2 * width] = dot(delta, w_in[...], 1, 1).astype(BF)
            lane = lane_ids((TILE, LANES)) == expert
            sent[at, 2 * width :] = jnp.where(lane, share, 0.0).astype(BF)
        if tick is not None:
            tick(i)
        return carry

    lax.fori_loop(0, CAP_PAD // TILE, tile, 0)


def return_rows(expert, held_col, sent, total, fresh, final, after):
    def image(i, carry):
        at = image_rows(i)
        column = held_col[at, :]
        column = jnp.sum(
            jnp.where(lane_ids(column.shape) == expert, column, 0), axis=1, keepdims=True
        )
        pick = jnp.where(lane_ids((SEQ_PAD, CAP_PAD)) == column, 1.0, 0.0).astype(BF)
        back = dot(pick, sent[...])
        if final is None:
            total[at, :] = back if fresh else total[at, :] + back
        else:
            back = back + total[at, :]
            start = 0
            for ref in final:
                ref[at, :] = back[:, start : start + ref.shape[1]].astype(BF)
                start += ref.shape[1]
        if after is not None:
            after(i)
        return carry

    lax.fori_loop(0, total.shape[0] // SEQ_PAD, image, 0)


def weight_rows(left, right, final, start, after):
    def step(i, carry):
        rows = pl.ds(pl.multiple_of(i * 256, 256), 256)
        to = pl.ds(pl.multiple_of(start + i * 256, 256), 256)
        final[to, :] = dot(left[:, rows], right[...], 0, 0).astype(BF)
        if after is not None:
            after(i)
        return carry

    lax.fori_loop(0, left.shape[1] // 256, step, 0)


def backward_image(
    i, images, attended, cotangent, sums, gate_sums, qkv, mixed, w_qkv, w_proj, w_router,
    gain_one, gain_two, partial, grad_hidden, grad_dense, grad_small,
):
    width = images.shape[1]
    at = image_rows(i)
    router = w_router[...]
    rows = images[at, :].astype(F32)
    plain, root = standardize(rows + attended[at, :].astype(F32))
    normed = (plain * gain_two[...]).astype(BF)
    gates = softmax_of(dot(normed, router, 1, 1), 1)
    grad_gates = gate_sums[at, :].astype(F32)[:, :8]
    grad_logits = gates * (grad_gates - jnp.sum(gates * grad_gates, axis=-1, keepdims=True))
    high = grad_logits.astype(BF)
    low = (grad_logits - high.astype(F32)).astype(BF)
    delta = sums[at, :].astype(F32) + (dot(high, router) + dot(low, router))
    grad_small[0:8, :] += dot(high, normed, 0, 0) + dot(low, normed, 0, 0)
    grad_small[8:9, :] += jnp.sum(delta * plain, axis=0, keepdims=True)
    grad = cotangent[at, :].astype(F32) + norm_back(delta, plain, root, gain_two[...])
    grad_hidden[at, :width] = grad
    grad = grad.astype(BF)
    grad_dense[3] += dot(mixed[at, :], grad, 0, 0)
    grad_mixed = dot(grad, w_proj[...], 1, 1).astype(BF)
    query, key, value = (qkv[s, at, :] for s in range(3))
    parts = [jnp.zeros(query.shape, F32) for _ in range(3)]
    for head in range(query.shape[1] // HD):
        mask = head_mask(query.shape, head)
        weights = attend(query, key, head)
        alone = jnp.where(mask, grad_mixed, jnp.zeros_like(grad_mixed))
        grad_weights = dot(alone, value, 1, 1)
        center = jnp.sum(weights * grad_weights, axis=-1, keepdims=True)
        scores = (weights * (grad_weights - center)).astype(BF)
        parts[0] = jnp.where(mask, dot(scores, key) * SCALE, parts[0])
        parts[1] = jnp.where(mask, dot(scores, query, 0, 0) * SCALE, parts[1])
        parts[2] = jnp.where(mask, dot(weights.astype(BF), grad_mixed, 0, 0), parts[2])
    first, _ = standardize(rows)
    first = (first * gain_one[...]).astype(BF)
    back = jnp.zeros((SEQ_PAD, width), F32)
    for s in range(3):
        part = parts[s].astype(BF)
        grad_dense[s] += dot(part, first, 0, 0)
        back = back + dot(part, w_qkv[s], 1, 1)
    partial[at, :] = back.astype(BF)


def output_image(i, images, attended, moe, output):
    at = image_rows(i)
    hidden = images[at, :].astype(F32) + attended[at, :].astype(F32)
    output[at, :] = (hidden + moe[at, :].astype(F32)).astype(BF)


def last_image(i, images, sums, grad_hidden, gain, grad_images, start, grad_gain):
    width = images.shape[1]
    at = image_rows(i)
    plain, root = standardize(images[at, :].astype(F32))
    delta = sums[at, :].astype(F32)
    grad_gain[0:1, :] += jnp.sum(delta * plain, axis=0, keepdims=True)
    grad = grad_hidden[at, :width] + norm_back(delta, plain, root, gain[...])
    grad_images[at, start : start + width] = grad


def loop(count, body):
    def step(i, carry):
        body(i)
        return carry

    lax.fori_loop(0, count, step, 0)


def attention_kernel(images, w_qkv, w_proj, gain, partial, qkv, mixed):
    loop(
        images.shape[0] // SEQ_PAD,
        lambda i: attention_image(i, images, w_qkv, w_proj, gain, partial, qkv, mixed),
    )


def second_norm_kernel(images, attended, gain, normed):
    loop(
        images.shape[0] // SEQ_PAD, lambda i: second_norm_image(i, images, attended, gain, normed)
    )


def expert_kernel(
    tokens, tokens_pair, back, back_pair, held, held_pair, held_col, w_router, w_in, w_out,
    moe, sums, gate_sums, main,
    gates, gates_pair, slots, inner, active, grads, sent, total,
):
    x = lax.rem(lax.axis_index("dp"), 2)
    gates[...] = softmax_of(dot(w_router[...], tokens[...], 1, 1), 0)
    gates_pair[...] = softmax_of(dot(w_router[...], tokens_pair[...], 1, 1), 0)
    width = tokens.shape[1]
    factors = (slots, inner, active, grads)
    for k in range(SPECIALIST_TOTAL):
        expert = lax.rem(x + k // PAIRED, 2) * PAIRED + k % PAIRED
        weights = (w_in.at[expert], w_out.at[expert])
        mine = factors if k < PAIRED else None
        expert_rows(expert, tokens, back, held, gates, *weights, mine, 0, sent, None)
        final = (moe, sums, gate_sums) if k == SPECIALIST_TOTAL - 1 else None
        return_rows(expert, held_col, sent, total, k == 0, final, None)
        if k < PAIRED:
            expert_rows(
                expert, tokens_pair, back_pair, held_pair, gates_pair, *weights, mine, CAP_PAD, None, None
            )
            weight_rows(slots, inner, main, 2 * k * width, None)
            weight_rows(active, grads, main, (2 * k + 1) * width, None)


def backward_kernel(
    images, attended, cotangent, moe, sums, gate_sums, qkv, mixed, w_qkv, w_proj, w_router,
    gain_one, gain_two,
    output, partial, grad_hidden, grad_dense, grad_small,
):
    grad_dense[...] = jnp.zeros_like(grad_dense)
    grad_small[...] = jnp.zeros_like(grad_small)

    def image(i):
        backward_image(
            i, images, attended, cotangent, sums, gate_sums, qkv, mixed, w_qkv, w_proj, w_router,
            gain_one, gain_two, partial, grad_hidden, grad_dense, grad_small,
        )
        output_image(i, images, attended, moe, output)

    loop(images.shape[0] // SEQ_PAD, image)


def last_kernel(images, sums, grad_hidden, gain, grad_images, grad_gain):
    grad_gain[...] = jnp.zeros_like(grad_gain)
    loop(
        images.shape[0] // SEQ_PAD,
        lambda i: last_image(i, images, sums, grad_hidden, gain, grad_images, 0, grad_gain),
    )


def call(kernel, outs, scratch, *args, flops=0):
    vmem = pl.BlockSpec(memory_space=pltpu.VMEM)
    return pl.pallas_call(
        kernel,
        out_shape=tuple(jax.ShapeDtypeStruct(shape, kind) for shape, kind in outs),
        in_specs=[vmem] * len(args),
        out_specs=tuple(vmem for _ in outs),
        scratch_shapes=[pltpu.VMEM(shape, kind) for shape, kind in scratch],
        compiler_params=pltpu.CompilerParams(vmem_limit_bytes=VMEM_LIMIT),
        cost_estimate=pl.CostEstimate(flops=flops, bytes_accessed=10**7, transcendentals=0),
    )(*args)


def swap_sum(main, dense):
    n_dp = lax.axis_size("dp")
    x = lax.axis_index("dp") % 2

    def swap(value, step):
        return lax.ppermute(value, "dp", [(i, i ^ step) for i in range(n_dp)])

    gone = lax.dynamic_index_in_dim(dense, 1 - x, 0, keepdims=False)
    mine = lax.dynamic_index_in_dim(dense, x, 0, keepdims=False)
    joined = (mine.astype(F32) + swap(gone, 1).astype(F32)).astype(BF)
    total = jnp.concatenate([main, joined], axis=0)
    step = 2
    while step < n_dp:
        total = (total.astype(F32) + swap(total, step).astype(F32)).astype(BF)
        step *= 2
    other = swap(total, 1)
    return jnp.where(x == 0, jnp.stack([total, other]), jnp.stack([other, total]))


def plain_step(rows, back, held_row, held_col, w_qkv, w_proj, router, w_in, w_out, gain_one, gain_two):
    padded, width = rows.shape
    local = w_proj.shape[0]
    n_dp = lax.axis_size("dp")
    swap = [(i, i ^ 1) for i in range(n_dp)]
    flat = (padded, width)
    held_pair = lax.ppermute(held_row, "dp", swap)
    back_pair = lax.ppermute(back, "dp", swap)
    partial, qkv, mixed = call(
        attention_kernel,
        [(flat, BF), ((3, padded, local), BF), ((padded, local), BF)],
        [],
        rows, w_qkv, w_proj, gain_one,
    )
    attended = pair_sum(partial)
    (normed,) = call(second_norm_kernel, [(flat, BF)], [], rows, attended, gain_two)
    normed_pair = lax.ppermute(normed, "dp", swap)
    wide = 2 * width + LANES
    moe, sums, gate_sums, main = call(
        expert_kernel,
        [(flat, BF), (flat, BF), ((padded, LANES), BF), ((4 * width, width), BF)],
        [((8, padded), F32)] * 2
        + [((2 * CAP_PAD, width), BF)] * 4
        + [((CAP_PAD, wide), BF), ((padded, wide), F32)],
        normed, normed_pair, back, back_pair,
        held_row, held_pair, held_col, router, w_in, w_out,
    )
    moe = pair_sum(moe)
    sums = pair_sum(sums)
    gate_sums = pair_sum(jnp.concatenate([gate_sums, gate_sums], axis=-1))[:, :LANES]
    output, partial, grad_hidden, grad_dense, grad_small = call(
        backward_kernel,
        [(flat, BF), (flat, BF), (flat, F32), ((4, local, width), F32), ((16, width), F32)],
        [],
        rows, attended, back, moe, sums, gate_sums,
        qkv, mixed, w_qkv, w_proj, router, gain_one, gain_two,
    )
    grad_images, grad_gain = call(
        last_kernel,
        [(flat, F32), ((8, width), F32)],
        [],
        rows, pair_sum(partial), grad_hidden, gain_one,
    )
    dense = grad_dense.reshape(2, 2 * local, width)
    small = jnp.stack([grad_small, jnp.pad(grad_gain, ((0, 8), (0, 0)))])
    dense = jnp.concatenate([dense, small], axis=1).astype(BF)
    whole = swap_sum(main, dense)
    rows_main = main.shape[0]
    experts = whole[:, :rows_main].reshape(SPECIALIST_TOTAL, 2, width, width)
    return output, grad_images, experts[:, 0], experts[:, 1], whole[:, rows_main:]


(
    ATT_RS, ATT_Y, ATT_AG, Z_X, Z_CORE, D_RS, G_RS, D_Y, G_Y, D_AG,
    O_RS, O_Y, O_AG, B_RS, B_Y, B_AG, COT, DENSE,
) = range(18)


def step_kernel(
    images, cotangent, held, held_pair, held_col, w_qkv, w_proj, router, gain_one, gain_two, w_in, w_out,
    output, grad_images, out_in, out_out, out_dense,
    back_pair, tokens, tokens_pair, attended, partial, qkv, mixed,
    core_a, far_a, core_d, far_d, core_o, far_o, core_g, far_g, gate_part, gate_sum,
    gates, gates_pair, slots, inner, active, grads, sent, total, slot_in, slot_out,
    grad_dense, grad_small, grad_last, main, landed, middle_ring, dense, dense_x, dense_landed, dense_middle,
    sends, recvs, weight_sems, send_low, recv_low, send_mid, recv_mid, send_down, recv_down,
    send_pair, recv_pair, keep, out_sems,
):
    place = lax.axis_index("dp")
    spot = lax.axis_index("tensor")
    x = lax.rem(place, 2)
    z = place // 2
    c = lax.rem(spot, 2)
    y = spot // 2
    inside = jnp.logical_or(z == 1, z == 2)
    outside = jnp.logical_not(inside)
    core = {"tensor": spot + 1 - 2 * c}
    far = {"tensor": spot + 2 - 4 * y}
    pair = {"dp": place + 1 - 2 * x}
    line = {"dp": (z + 1 - 2 * lax.rem(z, 2)) * 2 + x}
    middle = {"dp": (3 - z) * 2 + x}
    width = images.shape[1]
    half = width // 2
    count = images.shape[0] // SEQ_PAD
    pieces = main.shape[0] // PIECE
    per_expert = 2 * width // PIECE
    mine = pl.ds(pl.multiple_of(c * half, LANES), half)
    other = pl.ds(pl.multiple_of((1 - c) * half, LANES), half)
    local = w_proj.shape[0]

    barrier = pltpu.get_barrier_semaphore()
    for peer in (core, far, pair, line):
        pl.semaphore_signal(barrier, inc=1, device_id=peer, device_id_type=MESH)

    @pl.when(inside)
    def _():
        pl.semaphore_signal(barrier, inc=1, device_id=middle, device_id_type=MESH)

    def load(k):
        expert = lax.rem(x + k // PAIRED, 2) * PAIRED + k % PAIRED
        return [
            pltpu.make_async_copy(w_in.at[expert], slot_in.at[k % 2], weight_sems.at[0, k % 2]),
            pltpu.make_async_copy(w_out.at[expert], slot_out.at[k % 2], weight_sems.at[1, k % 2]),
        ]

    for k in range(2):
        for copy in load(k):
            copy.start()
    grad_dense[...] = jnp.zeros_like(grad_dense)
    grad_small[...] = jnp.zeros_like(grad_small)
    grad_last[...] = jnp.zeros_like(grad_last)

    @pl.when(inside)
    def _():
        pl.semaphore_wait(barrier, 5)

    @pl.when(outside)
    def _():
        pl.semaphore_wait(barrier, 4)

    def remote(src, dst, send, recv, peer):
        return pltpu.make_async_remote_copy(
            src_ref=src, dst_ref=dst, send_sem=send, recv_sem=recv,
            device_id=peer, device_id_type=MESH,
        )

    def channel(k, i, src, dst, peer):
        return remote(src, dst, sends.at[k, i], recvs.at[k, i], peer)

    def rs_copy(k, i, part, got):
        return channel(k, i, part.at[image_rows(i), other], got.at[image_rows(i), :], core)

    def far_copy(k, i, part, got):
        return channel(k, i, part.at[image_rows(i), mine], got.at[image_rows(i), :], far)

    def give_copy(k, i, result):
        view = result.at[image_rows(i), mine]
        return channel(k, i, view, view, core)

    def join_core(ks, i, part, near, got):
        at = image_rows(i)
        rs_copy(ks[0], i, part, near).wait_recv()
        rows = part[at, mine].astype(F32) + near[at, :].astype(F32)
        part[at, mine] = rows.astype(BF)
        far_copy(ks[1], i, part, got).start()

    def join_far(ks, i, part, got, result):
        at = image_rows(i)
        far_copy(ks[1], i, part, got).wait_recv()
        rows = part[at, mine].astype(F32) + got[at, :].astype(F32)
        result[at, mine] = rows.astype(BF)
        give_copy(ks[2], i, result).start()

    def sent_all(ks, part, near, got, result):
        def wait(i):
            rs_copy(ks[0], i, part, near).wait_send()
            far_copy(ks[1], i, part, got).wait_send()
            give_copy(ks[2], i, result).wait_send()

        loop(count, wait)

    def staged(step, lag, body):
        i = step - lag

        @pl.when(jnp.logical_and(i >= 0, i < count))
        def _():
            body(i)

    cot_copy = channel(COT, 0, cotangent.at[:, mine], back_pair.at[:, mine], pair)
    cot_give = channel(COT, 1, back_pair.at[:, mine], back_pair.at[:, mine], core)
    cot_copy.start()

    att = (ATT_RS, ATT_Y, ATT_AG)

    def token_copy(i):
        at = image_rows(i)
        return channel(Z_X, i, tokens.at[at, mine], tokens_pair.at[at, mine], pair)

    def token_give(i):
        view = tokens_pair.at[image_rows(i), mine]
        return channel(Z_CORE, i, view, view, core)

    def attention_step(step):
        def first(i):
            attention_image(i, images, w_qkv, w_proj, gain_one, partial, qkv, mixed)
            rs_copy(ATT_RS, i, partial, core_a).start()

        def norm(i):
            give_copy(ATT_AG, i, attended).wait_recv()
            second_norm_image(i, images, attended, gain_two, tokens)
            token_copy(i).start()

        def give(i):
            token_copy(i).wait_recv()
            token_give(i).start()

        staged(step, 0, first)
        staged(step, 1, lambda i: join_core(att, i, partial, core_a, far_a))
        staged(step, 2, lambda i: join_far(att, i, partial, far_a, attended))
        staged(step, 3, norm)
        staged(step, 5, give)

    loop(count + 3, attention_step)
    gates[...] = softmax_of(dot(router[...], tokens[...], 1, 1), 0)

    def piece(n):
        if isinstance(n, int) and n >= pieces:
            start, size = DENSE_CUTS[n - pieces]
            at = pl.ds(start, size)
            views = [ref.at[at, :] for ref in (dense.at[x], dense_landed, dense_middle)]
            return views + [out_dense.at[x, at, :]]
        at = pl.ds(pl.multiple_of(n * PIECE, PIECE), PIECE)
        return [main.at[at, :], landed.at[at, :], middle_ring.at[lax.rem(n, RING)], None]

    def out_views(n):
        if isinstance(n, int) and n >= pieces:
            return [(None, piece(n)[3])]
        per_kind = width // PIECE
        expert = x * PAIRED + n // per_expert
        kind = lax.rem(n // per_kind, 2)
        at = pl.ds(pl.multiple_of(lax.rem(n, per_kind) * PIECE, PIECE), PIECE)
        return [(kind == 0, out_in.at[expert, at, :]), (kind == 1, out_out.at[expert, at, :])]

    def low_copy(n):
        own, got, _, _ = piece(n)
        return remote(own, got, send_low.at[n], recv_low.at[n], line)

    def mid_copy(n):
        own, _, got, _ = piece(n)
        return remote(own, got, send_mid.at[n], recv_mid.at[n], middle)

    def down_copy(n):
        _, done, _, _ = piece(n)
        return remote(done, done, send_down.at[n], recv_down.at[n], line)

    def each_out(n, act):
        done = piece(n)[1]
        for when, view in out_views(n):
            copies = (
                remote(done, view, send_pair.at[n], recv_pair.at[n], pair),
                pltpu.make_async_copy(done, view, keep.at[n]),
            )
            if when is None:
                act(*copies)
            else:
                pl.when(when)(functools.partial(act, *copies))

    def publish(n):
        def act(swap, own):
            swap.start()
            own.start()

        each_out(n, act)

    def add_piece(to, left, right):
        rows = to.shape[0]
        size = 64 if rows % 64 == 0 else 48 if rows % 48 == 0 else 16

        def add(i):
            at = pl.ds(pl.multiple_of(i * size, 16), size)
            to[at, :] = (left[at, :].astype(F32) + right[at, :].astype(F32)).astype(BF)

        loop(rows // size, add)

    last = pieces + len(DENSE_CUTS)

    def tick(n):
        def when(n, body):
            if isinstance(n, int):
                if 0 <= n < last:
                    body(n)
            else:
                pl.when(n >= 0)(functools.partial(body, n))

        def gather(n):
            own, got, _, _ = piece(n)
            low_copy(n).wait_recv()
            add_piece(own, own, got)
            mid_copy(n).start()

        def finish(n):
            own, done, got, _ = piece(n)
            mid_copy(n).wait_recv()
            add_piece(done, own, got)
            down_copy(n).start()
            publish(n)

        def forward(n):
            down_copy(n).wait_recv()
            publish(n)

        @pl.when(inside)
        def _():
            when(n, gather)
            when(n - 1, finish)

        @pl.when(outside)
        def _():
            when(n - 2, forward)

    def lift(n):
        @pl.when(outside)
        def _():
            low_copy(n).start()

    factors = (slots, inner, active, grads)
    turn = 0
    final = (grads.at[: count * SEQ_PAD], slots.at[: count * SEQ_PAD], gate_part)
    moe_part, sum_part, _ = final
    dee = (D_RS, D_Y, D_AG)
    oh = (O_RS, O_Y, O_AG)
    moe, sums = tokens_pair, back_pair

    def gate_near(i):
        at = image_rows(i)
        return channel(G_RS, i, gate_part.at[at, :], core_g.at[at, :], core)

    def gate_far(i):
        at = image_rows(i)
        return channel(G_Y, i, gate_sum.at[at, :], far_g.at[at, :], far)

    def send_parts(i):
        rs_copy(D_RS, i, sum_part, core_d).start()
        gate_near(i).start()
        rs_copy(O_RS, i, moe_part, core_o).start()

    for k in range(SPECIALIST_TOTAL):
        expert = lax.rem(x + k // PAIRED, 2) * PAIRED + k % PAIRED
        weights = (slot_in.at[k % 2], slot_out.at[k % 2])
        for copy in load(k):
            copy.wait()
        kept = factors if k < PAIRED else None
        base = turn
        expert_rows(
            expert, tokens, cotangent, held, gates, *weights, kept, 0, sent,
            (lambda i, base=base: tick(base + i)) if k else None,
        )
        if k:
            turn += 2
        ends = k == SPECIALIST_TOTAL - 1
        return_rows(
            expert, held_col, sent, total, k == 0, final if ends else None,
            send_parts if ends else None,
        )
        if k:
            tick(turn)
            turn += 1
        if k == 0:
            cot_copy.wait_recv()
            cot_give.start()
            for i in range(count - 2, count):
                token_copy(i).wait_recv()
                token_give(i).start()
            loop(count, lambda i: token_give(i).wait_recv())
            cot_give.wait_recv()
            gates_pair[...] = softmax_of(dot(router[...], tokens_pair[...], 1, 1), 0)
            cot_copy.wait_send()
            cot_give.wait_send()
        if k < PAIRED:
            base = turn
            expert_rows(
                expert, tokens_pair, back_pair, held_pair, gates_pair, *weights, kept, CAP_PAD, None,
                (lambda i, base=base: tick(base + i)) if k else None,
            )
            if k:
                turn += 2
            for copy in load(k + 2):
                copy.start()
            per_step = 256 // PIECE
            for kind, (left, right) in enumerate(((slots, inner), (active, grads))):
                first = k * per_expert + kind * (width // PIECE)

                def after(i, first=first):
                    for j in range(per_step):
                        lift(first + i * per_step + j)

                weight_rows(left, right, main, (2 * k + kind) * width, after)
        if k == PAIRED - 1:

            def tokens_sent(i):
                token_copy(i).wait_send()
                token_give(i).wait_send()

            loop(count, tokens_sent)
            sent_all(att, partial, core_a, far_a, attended)

    bee = (B_RS, B_Y, B_AG)

    def backward_step(step):
        def gates_core(i):
            join_core(dee, i, sum_part, core_d, far_d)
            at = image_rows(i)
            gate_near(i).wait_recv()
            rows = gate_part[at, :].astype(F32) + core_g[at, :].astype(F32)
            gate_sum[at, :] = rows.astype(BF)
            gate_far(i).start()

        def gates_all(i):
            join_far(dee, i, sum_part, far_d, sums)
            at = image_rows(i)
            gate_far(i).wait()
            rows = gate_sum[at, :].astype(F32) + far_g[at, :].astype(F32)
            gate_sum[at, :] = rows.astype(BF)

        def back(i):
            give_copy(D_AG, i, sums).wait()
            backward_image(
                i, images, attended, cotangent, sums, gate_sum, qkv, mixed, w_qkv, w_proj, router,
                gain_one, gain_two, partial, total, grad_dense, grad_small,
            )
            rs_copy(B_RS, i, partial, core_a).start()

        def finish(i):
            give_copy(B_AG, i, sums).wait_recv()
            last_image(i, images, sums, total, gain_one, total, width, grad_last)
            grads_out(i).start()

        def emit(i):
            give_copy(O_AG, i, moe).wait()
            output_image(i, images, attended, moe, moe)
            rows_out(i).start()

        staged(step, 0, gates_core)
        staged(step, 1, gates_all)
        staged(step, 2, back)
        staged(step, 3, lambda i: join_core(bee, i, partial, core_a, far_a))
        staged(step, 4, lambda i: join_core(oh, i, moe_part, core_o, far_o))
        staged(step, 4, lambda i: join_far(bee, i, partial, far_a, sums))
        staged(step, 5, finish)
        staged(step, 5, lambda i: join_far(oh, i, moe_part, far_o, moe))
        staged(step, 6, emit)

    def grads_out(i):
        at = image_rows(i)
        return pltpu.make_async_copy(
            total.at[at, pl.ds(width, width)], grad_images.at[at, :], out_sems.at[0, i]
        )

    def rows_out(i):
        at = image_rows(i)
        return pltpu.make_async_copy(moe.at[at, :], output.at[at, :], out_sems.at[1, i])

    base = turn
    steps = count + 6

    def backward_turn(step):
        backward_step(step)
        tick(base + step)

    loop(steps, backward_turn)
    turn += steps

    def pack(i):
        at = pl.ds(pl.multiple_of(i * local, 16), local)
        dense[i // 2, pl.ds(pl.multiple_of(lax.rem(i, 2) * local, 16), local), :] = grad_dense[
            i
        ].astype(BF)

    loop(4, pack)
    dense[0, 2 * local : 2 * local + 16, :] = grad_small[...].astype(BF)
    dense[1, 2 * local : 2 * local + 16, :] = grad_last[...].astype(BF)

    def dense_copy(i):
        start, size = DENSE_CUTS[i]
        at = pl.ds(start, size)
        return channel(DENSE, i, dense.at[1 - x, at, :], dense_x.at[at, :], pair)

    cuts = range(len(DENSE_CUTS))
    for i in cuts:
        dense_copy(i).start()
    dense_from = min(turn + 4, pieces)
    while turn < dense_from:
        tick(turn)
        turn += 1
    for i in cuts:
        start, size = DENSE_CUTS[i]
        at = pl.ds(start, size)
        dense_copy(i).wait()
        dense[x, at, :] = (dense[x, at, :].astype(F32) + dense_x[at, :].astype(F32)).astype(BF)
        lift(pieces + i)
    while turn < last + 2:
        tick(turn)
        turn += 1

    def rest(i):
        rs_copy(D_RS, i, sum_part, core_d).wait_send()
        far_copy(D_Y, i, sum_part, far_d).wait_send()
        gate_near(i).wait_send()
        rs_copy(O_RS, i, moe_part, core_o).wait_send()
        far_copy(O_Y, i, moe_part, far_o).wait_send()
        grads_out(i).wait()
        rows_out(i).wait()

    loop(count, rest)
    sent_all(bee, partial, core_a, far_a, sums)

    def settle(n):
        @pl.when(outside)
        def _():
            low_copy(n).wait_send()

        @pl.when(inside)
        def _():
            mid_copy(n).wait_send()
            down_copy(n).wait_send()

        def act(swap, own):
            swap.wait()
            own.wait()

        each_out(n, act)

    loop(pieces, settle)
    for n in range(pieces, last):
        settle(n)


def eight_step(rows, back, held_row, held_col, w_qkv, w_proj, router, w_in, w_out, gain_one, gain_two):
    padded, width = rows.shape
    local = w_proj.shape[0]
    count = padded // SEQ_PAD
    n_dp = lax.axis_size("dp")
    held_pair = lax.ppermute(held_row, "dp", [(i, i ^ 1) for i in range(n_dp)])
    half = width // 2
    wide = 2 * width + LANES
    pieces = 4 * width // PIECE
    last = pieces + len(DENSE_CUTS)
    vmem = pl.BlockSpec(memory_space=pltpu.VMEM)
    hbm = pl.BlockSpec(memory_space=pl.ANY)
    flat = ((padded, width), BF)
    part = ((padded, half), BF)
    thin = ((padded, LANES), BF)
    square = (width, width)
    dense = ((DENSE_HALF, width), BF)
    scratch = [flat] * 5 + [((3, padded, local), BF), ((padded, local), BF)]
    scratch += [part] * 6 + [thin] * 4
    scratch += [((8, padded), F32)] * 2 + [((2 * CAP_PAD, width), BF)] * 4
    scratch += [((CAP_PAD, wide), BF), ((padded, wide), F32), ((2, *square), BF), ((2, *square), BF)]
    scratch += [((4, local, width), F32)] + [((16, width), F32)] * 2
    scratch += [((4 * width, width), BF)] * 2 + [((RING, PIECE, width), BF)]
    scratch += [((2, DENSE_HALF, width), BF)] + [dense] * 3
    dma = pltpu.SemaphoreType.DMA
    sems = [dma((18, count))] * 2 + [dma((2, 2))] + [dma((last,))] * 9 + [dma((2, count))]
    outs = [(flat[0], BF), (flat[0], F32)] + [((SPECIALIST_TOTAL, *square), BF)] * 2
    outs += [((2, DENSE_HALF, width), BF)]
    return pl.pallas_call(
        step_kernel,
        out_shape=tuple(jax.ShapeDtypeStruct(shape, kind) for shape, kind in outs),
        in_specs=[vmem] * 10 + [hbm] * 2,
        out_specs=tuple(hbm for _ in outs),
        scratch_shapes=[pltpu.VMEM(shape, kind) for shape, kind in scratch] + sems,
        compiler_params=pltpu.CompilerParams(
            collective_id=0, has_side_effects=True, vmem_limit_bytes=VMEM_LIMIT
        ),
        cost_estimate=pl.CostEstimate(flops=6 * 10**10, bytes_accessed=10**8, transcendentals=0),
    )(
        rows, back, held_row, held_pair, held_col, w_qkv, w_proj, router, gain_one, gain_two, w_in, w_out
    )


def per_device(
    images,
    w_qkv,
    w_proj,
    w_router,
    w_in,
    w_out,
    gain_one,
    gain_two,
    routes,
    order,
    counts,
    cotangent,
):
    img_count, seq_len, width = images.shape
    tokens = img_count * seq_len
    local = w_proj.shape[0]
    routes_g = routes.reshape(tokens, TOPK)
    held, kept_pairs = route_slots(routes_g, order[0], counts[0])
    held = jnp.pad(
        held.reshape(img_count, seq_len, SPECIALIST_TOTAL),
        ((0, 0), (0, SEQ_PAD - seq_len), (0, LANES - SPECIALIST_TOTAL)),
        constant_values=-1,
    )
    padded = img_count * SEQ_PAD
    held_col = held.reshape(padded, LANES)
    held_row = held_col[:, :8].T
    pads = ((0, 0), (0, SEQ_PAD - seq_len), (0, 0))
    rows = jnp.pad(images, pads).reshape(padded, width)
    back = jnp.pad(cotangent, pads).reshape(padded, width)
    router = jnp.pad(w_router.T, ((0, 8 - SPECIALIST_TOTAL), (0, 0)))
    step = eight_step if lax.axis_size("dp") == 8 else plain_step
    output, grad_images, grad_in, grad_out, dense = step(
        rows, back, held_row, held_col, w_qkv, w_proj, router, w_in, w_out,
        gain_one[None], gain_two[None],
    )
    cube = (img_count, SEQ_PAD, width)
    dense = dense.astype(F32)
    grads = dense[:, : 2 * local].reshape(4, local, width)
    return (
        output.reshape(cube)[:, :seq_len],
        grad_images.reshape(cube)[:, :seq_len],
        grads[:3].transpose(0, 2, 1),
        grads[3],
        dense[0, 2 * local : 2 * local + SPECIALIST_TOTAL].T,
        grad_in.astype(F32),
        grad_out.astype(F32),
        dense[1, 2 * local],
        dense[0, 2 * local + 8],
        kept_pairs.reshape(img_count, seq_len, TOPK),
    )


def solution(mesh):
    return jax.shard_map(
        per_device,
        mesh=mesh,
        in_specs=(
            P("dp", None, None),
            P(None, None, "tensor"),
            P("tensor", None),
            P(),
            P(None, None, "tensor"),
            P(None, "tensor", None),
            P(),
            P(),
            P("dp", None, None),
            P("dp", None),
            P("dp"),
            P("dp", None, None),
        ),
        out_specs=(
            P("dp", None, None),
            P("dp", None, None),
            P(None, None, "tensor"),
            P("tensor", None),
            P(),
            P(None, None, "tensor"),
            P(None, "tensor", None),
            P(),
            P(),
            P("dp", None, None),
        ),
        check_vma=False,
    )
```

time: 856 us -> 269 us (0.31)
  waiting for transfers between devices: 568 us -> 0.01 us
  Pallas kernels: 0 us -> 236 us
  matrix products: 117 us -> 0.84 us
  local copies, waits for them, and re-layouts: 62 us -> 16.5 us
  blocking collectives: 44.7 us -> 0 us
  other arithmetic: 40.8 us -> 10.8 us
  between operations: 16.3 us -> 1.52 us
    reduce_scatter x2 -> x0, waiting for transfers between devices: 296 us -> none  [the longest x1 164 us: reduce_experts(): lax.psum_scatter(grad_w_out, 'dp', scatter_dimension=2, tiled=True)]
    pallas_call x0 -> x1, Pallas kernels: none -> 236 us  [eight_step(): pl.pallas_call(step_kernel, out_shape=tuple((jax.ShapeDtypeStruct(shape,...]
    psum x4 -> x0, waiting for transfers between devices: 172 us -> none  [the longest x1 104 us: per_device(): lax.psum((grad_qkv, grad_proj, grad_router, grad_gain_one, grad_gain_two)...]
    dot_general x24 -> x1, matrix products: 114 us -> 0.84 us  [route_slots(): before = jnp.dot(earlier, marks.astype(BF), preferred_element_type=F32)]
    all_gather x2 -> x0, waiting for transfers between devices: 99.9 us -> none  [the longest x1 73.6 us: reduce_experts(): lax.all_gather(share_out.astype(jnp.bfloat16), 'dp', axis=2, tiled=True)]
    psum x2 -> x0, blocking collectives: 44.7 us -> none  [the longest x1 38.8 us: per_device(): lax.psum((grad_qkv, grad_proj, grad_router, grad_gain_one, grad_gain_two)...]
    reduce_sum x14 -> x2, other arithmetic: 18.8 us -> 1.3 us  [the longest x1 1.18 us: route_slots(): place = jnp.sum(jnp.where(spots, positions[:, None], 0), axis=0)]
    gather x6 -> x0, local copies, waits for them, and re-layouts: 14.6 us -> none  [the longest x1 4.53 us: route_slots(): alive_rows = in_image[order_g]]
  transfers between devices with their start and end apart: 8 -> 1, of which waited for: 7 -> 0; matrix products, arithmetic and copies ran while one was open for 18% -> 2% of each run, Pallas kernels for 0% -> 0%
where the time goes in v1:
time: 269 us
  Pallas kernels  236 us (88%)
  local copies, waits for them, and re-layouts  16.5 us (6%)
  other arithmetic  10.8 us (4%)
  starting transfers between devices  2.99 us (1%)
    pallas_call x1, Pallas kernels, eight_step(): pl.pallas_call(step_kernel, out_shape=tuple((jax.ShapeDtypeStruct(shape,...  236 us
  transfers between devices with their start and end apart: 1, of which 0 were waited for; matrix products, arithmetic and copies ran while one was open for 2% of the time, Pallas kernels for 0%

profile of v1, /device:TPU:0, one launch (start us, length us, event | category | flops | bytes accessed | tf_op | source)
XLA Modules:
  0.0 268.8 jit_solution(3352374635465836146)
XLA Ops:
  1.3 0.1 eq.51
  1.4 1.2 select_reduce_fusion
  2.6 0.7 copy.37
  3.3 0.0 copy-start.9
  3.3 0.1 eq.41
  3.4 0.0 copy-start.10
  3.4 0.0 copy-start.6
  3.4 0.1 slice_reduce_fusion
  3.6 0.1 fusion.12
  3.7 0.8 multiply_reduce_fusion
  4.6 0.1 reshape.113
  4.7 0.2 copy.43
  4.9 0.0 copy-start.8
  4.9 0.0 copy-start.3
  5.0 0.0 copy-start.2
  5.1 0.2 copy.40.held
  5.2 0.0 copy-start.7
  5.2 3.0 %collective-permute-start = (s32[8,1040]{1,0:T(8,128)S(1)}, s32[8,1040]{1,0:T(8,128)S(1)}, u32[]{:S(2)}, u32[]{:S(2)}) collective-permute-start(s32[8,1040]{1,0:T(8,128)S(1)} %copy.40.held), channel_id=1, source_target_pairs={{0,4},{4,0},{8,12},{12,8},{16,20},{20,16},{24,28},{28,24},{1,5},{5... | collective-permute-start | bytes 99848 | tf_op jit(solution)/shard_map/ppermute | solution.py:916
  8.2 0.1 lt.53
  8.4 0.0 copy-done.9
  8.4 0.6 broadcast_in_dim.34.gain_one
  8.9 0.0 copy-done.10
  8.9 0.6 broadcast_in_dim.35.gain_two
  9.5 0.6 copy.42
  10.1 0.0 copy-done.6
  10.1 1.4 copy.41.w_qkv
  11.5 0.0 copy-start.4
  11.6 0.0 copy-done.8
  11.6 0.6 pad.19.router
  12.2 0.0 copy-done.3
  12.2 1.3 pad.16
  13.4 0.0 copy-done.2
  13.4 0.0 copy-done.7
  13.4 0.0 copy-done.4
  13.4 1.3 pad.17
  14.7 0.0 collective-permute-done.held_pair
  14.7 0.0 copy-start.11
  14.7 0.6 copy-done.11
  15.3 236.2 %shard_map.195 = (bf16[1040,768]{1,0:T(8,128)(2,1)}, f32[1040,768]{1,0:T(8,128)}, bf16[4,768,768]{2,1,0:T(8,128)(2,1)}, bf16[4,768,768]{2,1,0:T(8,128)(2,1)}, bf16[2,400,768]{2,1,0:T(8,128)(2,1)}) custom-call(bf16[1040,768]{1,0:T(8,128)(2,1)} %bitcast.52, bf16[1040,768]{1,0:T(8,128)(2,1)} %bitcast.53, s32[8,1040]{1,0:T(8,128)} %copy-done.7, ...), custom_call_target="tpu_custom_call" | custom-call | flops 60000002048 | bytes 100000000 | tf_op jit(solution)/shard_map/pallas_call | solution.py:939
  251.5 1.4 slice.44
  252.9 0.0 copy-start
  253.0 0.9 slice_bitcast_fusion.1
  253.8 0.0 copy-start.5
  253.8 0.0 copy-start.1
  253.8 1.3 slice_bitcast_fusion
  255.1 0.0 copy-done
  255.1 0.0 slice-start.2
  255.1 0.2 convert_element_type.40
  255.3 0.6 slice_reduce_fusion.1
  255.9 0.6 slice_bitcast_fusion.3
  256.5 0.0 copy-done.5
  256.5 0.0 slice-start.3
  256.5 1.2 slice.42
  257.8 0.0 copy-done.1
  257.8 0.0 slice-start
  257.8 1.9 slice.43
  259.7 0.0 slice-done.2
  259.7 0.0 slice-done.3
  259.7 0.0 slice-start.1
  259.7 4.6 %convert_element_type.41 = f32[4,768,768]{2,1,0:T(8,128)} convert(bf16[4,768,768]{2,1,0:T(8,128)(2,1)S(1)} %bitcast.48) | non-fusion elementwise | flops 2359296 | bytes 14155776 | tf_op jit(solution)/shard_map/convert_element_type | solution.py:999
  264.3 0.0 slice-done
  264.3 0.0 slice-done.1
  264.3 4.6 %convert_element_type.42 = f32[4,768,768]{2,1,0:T(8,128)} convert(bf16[4,768,768]{2,1,0:T(8,128)(2,1)S(1)} %bitcast.46) | non-fusion elementwise | flops 2359296 | bytes 14155776 | tf_op jit(solution)/shard_map/convert_element_type | solution.py:1000
  (15 shorter events, 0.2 us)
Async XLA Ops:
  3.3 5.0 %copy-start.9 = (f32[768]{0:T(1024)S(1)}, f32[768]{0:T(1024)}, u32[]{:S(2)}) copy-start(f32[768]{0:T(1024)} %param.18) | copy-start | bytes 9220
  3.4 5.5 %copy-start.10 = (f32[768]{0:T(1024)S(1)}, f32[768]{0:T(1024)}, u32[]{:S(2)}) copy-start(f32[768]{0:T(1024)} %param.19) | copy-start | bytes 9220
  3.4 6.7 %copy-start.6 = (bf16[3,768,192]{1,2,0:T(8,128)(2,1)S(1)}, bf16[3,768,192]{1,2,0:T(8,128)(2,1)}, u32[]{:S(2)}) copy-start(bf16[3,768,192]{1,2,0:T(8,128)(2,1)} %param.13) | copy-start | bytes 2654212
  4.9 6.6 %copy-start.8 = (bf16[768,4]{0,1:T(4,128)(2,1)S(1)}, bf16[768,4]{0,1:T(4,128)(2,1)}, u32[]{:S(2)}) copy-start(bf16[768,4]{0,1:T(4,128)(2,1)} %param.15) | copy-start | bytes 18436
  4.9 7.2 %copy-start.3 = (bf16[5,197,768]{2,1,0:T(8,128)(2,1)S(1)}, bf16[5,197,768]{2,1,0:T(8,128)(2,1)}, u32[]{:S(2)}) copy-start(bf16[5,197,768]{2,1,0:T(8,128)(2,1)} %param.12) | copy-start | bytes 4538884
  5.0 8.4 %copy-start.2 = (s32[5,208,128]{2,1,0:T(8,128)}, s32[5,208,128]{2,1,0:T(8,128)S(1)}, u32[]{:S(2)}) copy-start(s32[5,208,128]{2,1,0:T(8,128)S(1)} %pad.18.clone) | copy-start | bytes 1597444
  5.2 8.2 %copy-start.7 = (s32[8,1040]{1,0:T(8,128)}, s32[8,1040]{1,0:T(8,128)S(1)}, u32[]{:S(2)}) copy-start(s32[8,1040]{1,0:T(8,128)S(1)} %copy.40.held) | copy-start | bytes 99844
  5.2 9.4 %collective-permute-start = (s32[8,1040]{1,0:T(8,128)S(1)}, s32[8,1040]{1,0:T(8,128)S(1)}, u32[]{:S(2)}, u32[]{:S(2)}) collective-permute-start(s32[8,1040]{1,0:T(8,128)S(1)} %copy.40.held), channel_id=1, source_target_pairs={{0,4},{4,0},{8,12},{12,8},{16,20},{20,16},{24,28},{28,24},{1,5},{5... | collective-permute-start | bytes 99848 | tf_op jit(solution)/shard_map/ppermute | solution.py:916
  11.5 1.9 copy-start.4
  14.7 0.6 copy-start.11
  252.9 2.2 copy-start
  253.8 2.7 %copy-start.5 = (bf16[1040,768]{1,0:T(8,128)(2,1)S(1)}, bf16[1040,768]{1,0:T(8,128)(2,1)}, u32[]{:S(2)}) copy-start(bf16[1040,768]{1,0:T(8,128)(2,1)} %get-tuple-element.15) | copy-start | bytes 4792324
  253.8 4.0 %copy-start.1 = (f32[1040,768]{1,0:T(8,128)S(1)}, f32[1040,768]{1,0:T(8,128)}, u32[]{:S(2)}) copy-start(f32[1040,768]{1,0:T(8,128)} %get-tuple-element.16) | copy-start | bytes 9584644
  255.1 4.5 %slice-start.2 = ((s8[4718592]{0:T(1024)(128)(4,1)}), s8[4194304]{0:T(1024)(128)(4,1)S(1)}, s32[]{:S(2)}) async-start(s8[4718592]{0:T(1024)(128)(4,1)} %bitcast.47), calls=%async_computation.2 | async-start | bytes 8388608
  256.5 3.1 %slice-start.3 = ((s8[4718592]{0:T(1024)(128)(4,1)}), s8[524288]{0:T(1024)(128)(4,1)S(1)}, s32[]{:S(2)}) async-start(s8[4718592]{0:T(1024)(128)(4,1)} %bitcast.47), calls=%async_computation.3 | async-start | bytes 1048576
  257.8 6.5 %slice-start = ((s8[4718592]{0:T(1024)(128)(4,1)}), s8[4194304]{0:T(1024)(128)(4,1)S(1)}, s32[]{:S(2)}) async-start(s8[4718592]{0:T(1024)(128)(4,1)} %bitcast.45), calls=%async_computation | async-start | bytes 8388608
  259.7 4.6 %slice-start.1 = ((s8[4718592]{0:T(1024)(128)(4,1)}), s8[524288]{0:T(1024)(128)(4,1)S(1)}, s32[]{:S(2)}) async-start(s8[4718592]{0:T(1024)(128)(4,1)} %bitcast.45), calls=%async_computation.1 | async-start | bytes 1048576

commit v2 on v1

--- a/solution.py
+++ b/solution.py
@@ -18,7 +18,8 @@
 PAIRED = SPECIALIST_TOTAL // 2
 LANES = 128
 PIECE = 128
-RING = 4
+RING = 6
+LAG = 2
 DENSE_CUTS = ((0, 96), (96, 96), (192, 96), (288, 96), (384, 16))
 DENSE_HALF = 400
 
@@ -121,7 +122,7 @@
     plain, _ = standardize(images[at, :].astype(F32))
     normed = (plain * gain[...]).astype(BF)
     for s in range(3):
-        qkv[s, at, :] = dot(normed, w_qkv[s]).astype(BF)
+        qkv[s, at, :] = dot(normed, w_qkv[s], 1, 1).astype(BF)
     query, key, value = (qkv[s, at, :] for s in range(3))
     result = jnp.zeros(query.shape, F32)
     for head in range(query.shape[1] // HD):
@@ -190,7 +191,7 @@
     lax.fori_loop(0, CAP_PAD // TILE, tile, 0)
 
 
-def return_rows(expert, held_col, sent, total, fresh, final, after):
+def return_rows(expert, held_col, sent, total, fresh, final, after, first=0, stop=None):
     def image(i, carry):
         at = image_rows(i)
         column = held_col[at, :]
@@ -211,7 +212,7 @@
             after(i)
         return carry
 
-    lax.fori_loop(0, total.shape[0] // SEQ_PAD, image, 0)
+    lax.fori_loop(first, stop or total.shape[0] // SEQ_PAD, image, 0)
 
 
 def weight_rows(left, right, final, start, after):
@@ -267,7 +268,7 @@
     for s in range(3):
         part = parts[s].astype(BF)
         grad_dense[s] += dot(part, first, 0, 0)
-        back = back + dot(part, w_qkv[s], 1, 1)
+        back = back + dot(part, w_qkv[s])
     partial[at, :] = back.astype(BF)
 
 
@@ -394,6 +395,7 @@
 def plain_step(rows, back, held_row, held_col, w_qkv, w_proj, router, w_in, w_out, gain_one, gain_two):
     padded, width = rows.shape
     local = w_proj.shape[0]
+    router = jnp.pad(router, ((0, 8 - SPECIALIST_TOTAL), (0, 0)))
     n_dp = lax.axis_size("dp")
     swap = [(i, i ^ 1) for i in range(n_dp)]
     flat = (padded, width)
@@ -440,22 +442,24 @@
     whole = swap_sum(main, dense)
     rows_main = main.shape[0]
     experts = whole[:, :rows_main].reshape(SPECIALIST_TOTAL, 2, width, width)
-    return output, grad_images, experts[:, 0], experts[:, 1], whole[:, rows_main:]
+    grads = whole[:, rows_main : rows_main + 2 * local].reshape(4, local, width)
+    small = whole[:, rows_main + 2 * local :]
+    return output, grad_images, experts[:, 0], experts[:, 1], grads, small
 
 
 (
     ATT_RS, ATT_Y, ATT_AG, Z_X, Z_CORE, D_RS, G_RS, D_Y, G_Y, D_AG,
-    O_RS, O_Y, O_AG, B_RS, B_Y, B_AG, COT, DENSE,
-) = range(18)
+    O_RS, O_Y, O_AG, B_RS, B_Y, B_AG, COT, COT_Y, COT_CORE, DENSE, HELD,
+) = range(21)
 
 
 def step_kernel(
-    images, cotangent, held, held_pair, held_col, w_qkv, w_proj, router, gain_one, gain_two, w_in, w_out,
-    output, grad_images, out_in, out_out, out_dense,
-    back_pair, tokens, tokens_pair, attended, partial, qkv, mixed,
+    images, cotangent, held, held_col, w_qkv, w_proj, vectors, w_in, w_out,
+    output, grad_images, out_in, out_out, out_grads, out_small,
+    held_pair, router, back_pair, tokens, tokens_pair, attended, partial, qkv, mixed,
     core_a, far_a, core_d, far_d, core_o, far_o, core_g, far_g, gate_part, gate_sum,
     gates, gates_pair, slots, inner, active, grads, sent, total, slot_in, slot_out,
-    grad_dense, grad_small, grad_last, main, landed, middle_ring, dense, dense_x, dense_landed, dense_middle,
+    grad_dense, grad_small, grad_last, main, landed, middle_ring, dense_x,
     sends, recvs, weight_sems, send_low, recv_low, send_mid, recv_mid, send_down, recv_down,
     send_pair, recv_pair, keep, out_sems,
 ):
@@ -480,6 +484,9 @@
     mine = pl.ds(pl.multiple_of(c * half, LANES), half)
     other = pl.ds(pl.multiple_of((1 - c) * half, LANES), half)
     local = w_proj.shape[0]
+    gain_one, gain_two = vectors.at[0:1], vectors.at[1:2]
+    dense = active
+    dense_landed, dense_middle = inner.at[:DENSE_HALF], inner.at[DENSE_HALF : 2 * DENSE_HALF]
 
     barrier = pltpu.get_barrier_semaphore()
     for peer in (core, far, pair, line):
@@ -499,6 +506,7 @@
     for k in range(2):
         for copy in load(k):
             copy.start()
+    router[...] = vectors[8:16, :].astype(BF)
     grad_dense[...] = jnp.zeros_like(grad_dense)
     grad_small[...] = jnp.zeros_like(grad_small)
     grad_last[...] = jnp.zeros_like(grad_last)
@@ -554,14 +562,65 @@
 
     def staged(step, lag, body):
         i = step - lag
+        if isinstance(i, int):
+            if 0 <= i < count:
+                body(i)
+            return
 
         @pl.when(jnp.logical_and(i >= 0, i < count))
         def _():
             body(i)
 
-    cot_copy = channel(COT, 0, cotangent.at[:, mine], back_pair.at[:, mine], pair)
-    cot_give = channel(COT, 1, back_pair.at[:, mine], back_pair.at[:, mine], core)
-    cot_copy.start()
+    held_copy = channel(HELD, 0, held, held_pair, pair)
+    held_copy.start()
+
+    def cot_copy(i):
+        at = image_rows(i)
+        return channel(COT, i, cotangent.at[at, mine], back_pair.at[at, mine], pair)
+
+    def cot_far(i):
+        view = back_pair.at[image_rows(i), mine]
+        return channel(COT_Y, i, view, view, far)
+
+    def cot_give(i):
+        view = back_pair.at[image_rows(i), mine]
+        return channel(COT_CORE, i, view, view, core)
+
+    def shared(i):
+        return i < count - 1
+
+    def direct(i):
+        return jnp.logical_or(lax.rem(i, 2) == y, i == count - 1)
+
+    def cot_send(i):
+        @pl.when(direct(i))
+        def _():
+            cot_copy(i).start()
+
+    def cot_pass(i):
+        @pl.when(direct(i))
+        def _():
+            cot_copy(i).wait()
+            cot_give(i).start()
+
+            @pl.when(shared(i))
+            def _():
+                cot_far(i).start()
+
+    def cot_land(i):
+        @pl.when(jnp.logical_not(direct(i)))
+        def _():
+            cot_far(i).wait_recv()
+            cot_give(i).start()
+
+    def cot_end(i):
+        cot_give(i).wait()
+
+        @pl.when(jnp.logical_and(direct(i), shared(i)))
+        def _():
+            cot_far(i).wait_send()
+
+    loop(count, cot_send)
 
     att = (ATT_RS, ATT_Y, ATT_AG)
 
@@ -583,25 +642,30 @@
             second_norm_image(i, images, attended, gain_two, tokens)
             token_copy(i).start()
 
-        def give(i):
-            token_copy(i).wait_recv()
-            token_give(i).start()
-
         staged(step, 0, first)
         staged(step, 1, lambda i: join_core(att, i, partial, core_a, far_a))
         staged(step, 2, lambda i: join_far(att, i, partial, far_a, attended))
         staged(step, 3, norm)
-        staged(step, 5, give)
+
+        @pl.when(step == count + 1)
+        def _():
+            loop(count, cot_pass)
 
     loop(count + 3, attention_step)
     gates[...] = softmax_of(dot(router[...], tokens[...], 1, 1), 0)
+
+    def dense_half(side):
+        return pl.ds(pl.multiple_of(side * DENSE_HALF, 16), DENSE_HALF)
 
     def piece(n):
         if isinstance(n, int) and n >= pieces:
             start, size = DENSE_CUTS[n - pieces]
             at = pl.ds(start, size)
-            views = [ref.at[at, :] for ref in (dense.at[x], dense_landed, dense_middle)]
-            return views + [out_dense.at[x, at, :]]
+            views = [ref.at[at, :] for ref in (dense.at[dense_half(x)], dense_landed, dense_middle)]
+            if size == 16:
+                return views + [out_small.at[x]]
+            at = pl.ds(start % local, size)
+            return views + [out_grads.at[2 * x + start // local, at, :]]
         at = pl.ds(pl.multiple_of(n * PIECE, PIECE), PIECE)
         return [main.at[at, :], landed.at[at, :], middle_ring.at[lax.rem(n, RING)], None]
 
@@ -685,11 +749,11 @@
         @pl.when(inside)
         def _():
             when(n, gather)
-            when(n - 1, finish)
+            when(n - LAG, finish)
 
         @pl.when(outside)
         def _():
-            when(n - 2, forward)
+            when(n - 2 * LAG, forward)
 
     def lift(n):
         @pl.when(outside)
@@ -731,24 +795,26 @@
         if k:
             turn += 2
         ends = k == SPECIALIST_TOTAL - 1
-        return_rows(
-            expert, held_col, sent, total, k == 0, final if ends else None,
-            send_parts if ends else None,
-        )
-        if k:
+        if k == 0:
+
+            def give(i):
+                token_copy(i).wait_recv()
+                token_give(i).start()
+
+            loop(count, give)
+            loop(count, cot_land)
+            return_rows(expert, held_col, sent, total, True, None, None, 0, 2)
+            loop(count, lambda i: token_give(i).wait_recv())
+            loop(count, cot_end)
+            held_copy.wait()
+            gates_pair[...] = softmax_of(dot(router[...], tokens_pair[...], 1, 1), 0)
+        else:
+            return_rows(
+                expert, held_col, sent, total, False, final if ends else None,
+                send_parts if ends else None,
+            )
             tick(turn)
             turn += 1
-        if k == 0:
-            cot_copy.wait_recv()
-            cot_give.start()
-            for i in range(count - 2, count):
-                token_copy(i).wait_recv()
-                token_give(i).start()
-            loop(count, lambda i: token_give(i).wait_recv())
-            cot_give.wait_recv()
-            gates_pair[...] = softmax_of(dot(router[...], tokens_pair[...], 1, 1), 0)
-            cot_copy.wait_send()
-            cot_give.wait_send()
         if k < PAIRED:
             base = turn
             expert_rows(
@@ -768,6 +834,10 @@
                         lift(first + i * per_step + j)
 
                 weight_rows(left, right, main, (2 * k + kind) * width, after)
+            if k == 0:
+                return_rows(expert, held_col, sent, total, True, None, None, 2)
+                tick(turn)
+                turn += 1
         if k == PAIRED - 1:
 
             def tokens_sent(i):
@@ -803,25 +873,12 @@
             )
             rs_copy(B_RS, i, partial, core_a).start()
 
-        def finish(i):
-            give_copy(B_AG, i, sums).wait_recv()
-            last_image(i, images, sums, total, gain_one, total, width, grad_last)
-            grads_out(i).start()
-
-        def emit(i):
-            give_copy(O_AG, i, moe).wait()
-            output_image(i, images, attended, moe, moe)
-            rows_out(i).start()
-
         staged(step, 0, gates_core)
         staged(step, 1, gates_all)
         staged(step, 2, back)
         staged(step, 3, lambda i: join_core(bee, i, partial, core_a, far_a))
-        staged(step, 4, lambda i: join_core(oh, i, moe_part, core_o, far_o))
         staged(step, 4, lambda i: join_far(bee, i, partial, far_a, sums))
         staged(step, 5, finish)
-        staged(step, 5, lambda i: join_far(oh, i, moe_part, far_o, moe))
-        staged(step, 6, emit)
 
     def grads_out(i):
         at = image_rows(i)
@@ -833,45 +890,74 @@
         at = image_rows(i)
         return pltpu.make_async_copy(moe.at[at, :], output.at[at, :], out_sems.at[1, i])
 
+    def finish(i):
+        give_copy(B_AG, i, sums).wait_recv()
+        last_image(i, images, sums, total, gain_one, total, width, grad_last)
+        grads_out(i).start()
+
+    def emit(i):
+        give_copy(O_AG, i, moe).wait()
+        output_image(i, images, attended, moe, moe)
+        rows_out(i).start()
+
     base = turn
-    steps = count + 6
 
     def backward_turn(step):
+        turns = base + step + jnp.maximum(step - 2, 0)
+        tick(turns)
         backward_step(step)
-        tick(base + step)
-
-    loop(steps, backward_turn)
-    turn += steps
+
+        @pl.when(step >= 2)
+        def _():
+            tick(turns + 1)
+
+    loop(count + 2, backward_turn)
+    turn += 2 * count + 2
 
     def pack(i):
-        at = pl.ds(pl.multiple_of(i * local, 16), local)
-        dense[i // 2, pl.ds(pl.multiple_of(lax.rem(i, 2) * local, 16), local), :] = grad_dense[
-            i
-        ].astype(BF)
-
+        start = i // 2 * DENSE_HALF + lax.rem(i, 2) * local
+        dense[pl.ds(pl.multiple_of(start, 16), local), :] = grad_dense[i].astype(BF)
+
+    def dense_view(i, side=0):
+        start, size = DENSE_CUTS[i]
+        return pl.ds(pl.multiple_of(side * DENSE_HALF + start, 16), size)
+
+    def dense_copy(i):
+        at = dense_view(i)
+        return channel(DENSE, i, dense.at[dense_view(i, 1 - x), :], dense_x.at[at, :], pair)
+
+    def dense_join(i):
+        at = dense_view(i)
+        dense_copy(i).wait()
+        own = dense_view(i, x)
+        dense[own, :] = (dense[own, :].astype(F32) + dense_x[at, :].astype(F32)).astype(BF)
+        lift(pieces + i)
+
+    small = len(DENSE_CUTS) - 1
     loop(4, pack)
-    dense[0, 2 * local : 2 * local + 16, :] = grad_small[...].astype(BF)
-    dense[1, 2 * local : 2 * local + 16, :] = grad_last[...].astype(BF)
-
-    def dense_copy(i):
-        start, size = DENSE_CUTS[i]
-        at = pl.ds(start, size)
-        return channel(DENSE, i, dense.at[1 - x, at, :], dense_x.at[at, :], pair)
-
-    cuts = range(len(DENSE_CUTS))
-    for i in cuts:
+    for i in range(small):
         dense_copy(i).start()
-    dense_from = min(turn + 4, pieces)
-    while turn < dense_from:
+    join_core(bee, count - 1, partial, core_a, far_a)
+    loop(count, lambda i: join_core(oh, i, moe_part, core_o, far_o))
+    while turn < pieces:
         tick(turn)
         turn += 1
-    for i in cuts:
-        start, size = DENSE_CUTS[i]
-        at = pl.ds(start, size)
-        dense_copy(i).wait()
-        dense[x, at, :] = (dense[x, at, :].astype(F32) + dense_x[at, :].astype(F32)).astype(BF)
-        lift(pieces + i)
-    while turn < last + 2:
+    for i in range(count - 2, count):
+        join_far(bee, i, partial, far_a, sums)
+        finish(i - 1)
+    finish(count - 1)
+    for side, rows in enumerate((grad_small, grad_last)):
+        dense[dense_view(small, side), :] = rows[...].astype(BF)
+    dense_copy(small).start()
+    for i in range(len(DENSE_CUTS)):
+        dense_join(i)
+        tick(turn)
+        turn += 1
+        join_far(oh, i, moe_part, far_o, moe)
+        if i:
+            emit(i - 1)
+    emit(count - 1)
+    while turn < last + 2 * LAG:
         tick(turn)
         turn += 1
 
@@ -912,9 +998,9 @@
     padded, width = rows.shape
     local = w_proj.shape[0]
     count = padded // SEQ_PAD
-    n_dp = lax.axis_size("dp")
-    held_pair = lax.ppermute(held_row, "dp", [(i, i ^ 1) for i in range(n_dp)])
     half = width // 2
+    gap = jnp.zeros((6, width), F32)
+    vectors = jnp.concatenate([gain_one, gain_two, gap, router.astype(F32), gap[:4]])
     wide = 2 * width + LANES
     pieces = 4 * width // PIECE
     last = pieces + len(DENSE_CUTS)
@@ -924,22 +1010,21 @@
     part = ((padded, half), BF)
     thin = ((padded, LANES), BF)
     square = (width, width)
-    dense = ((DENSE_HALF, width), BF)
-    scratch = [flat] * 5 + [((3, padded, local), BF), ((padded, local), BF)]
+    scratch = [((8, padded), jnp.int32), ((8, width), BF)] + [flat] * 5 + [((3, padded, local), BF), ((padded, local), BF)]
     scratch += [part] * 6 + [thin] * 4
     scratch += [((8, padded), F32)] * 2 + [((2 * CAP_PAD, width), BF)] * 4
     scratch += [((CAP_PAD, wide), BF), ((padded, wide), F32), ((2, *square), BF), ((2, *square), BF)]
     scratch += [((4, local, width), F32)] + [((16, width), F32)] * 2
     scratch += [((4 * width, width), BF)] * 2 + [((RING, PIECE, width), BF)]
-    scratch += [((2, DENSE_HALF, width), BF)] + [dense] * 3
+    scratch += [((DENSE_HALF, width), BF)]
     dma = pltpu.SemaphoreType.DMA
-    sems = [dma((18, count))] * 2 + [dma((2, 2))] + [dma((last,))] * 9 + [dma((2, count))]
+    sems = [dma((21, count))] * 2 + [dma((2, 2))] + [dma((last,))] * 9 + [dma((2, count))]
     outs = [(flat[0], BF), (flat[0], F32)] + [((SPECIALIST_TOTAL, *square), BF)] * 2
-    outs += [((2, DENSE_HALF, width), BF)]
+    outs += [((4, local, width), BF), ((2, 16, width), BF)]
     return pl.pallas_call(
         step_kernel,
         out_shape=tuple(jax.ShapeDtypeStruct(shape, kind) for shape, kind in outs),
-        in_specs=[vmem] * 10 + [hbm] * 2,
+        in_specs=[vmem] * 7 + [hbm] * 2,
         out_specs=tuple(hbm for _ in outs),
         scratch_shapes=[pltpu.VMEM(shape, kind) for shape, kind in scratch] + sems,
         compiler_params=pltpu.CompilerParams(
@@ -947,7 +1032,7 @@
         ),
         cost_estimate=pl.CostEstimate(flops=6 * 10**10, bytes_accessed=10**8, transcendentals=0),
     )(
-        rows, back, held_row, held_pair, held_col, w_qkv, w_proj, router, gain_one, gain_two, w_in, w_out
+        rows, back, held_row, held_col, w_qkv, w_proj, vectors, w_in, w_out
     )
 
 
@@ -967,7 +1052,6 @@
 ):
     img_count, seq_len, width = images.shape
     tokens = img_count * seq_len
-    local = w_proj.shape[0]
     routes_g = routes.reshape(tokens, TOPK)
     held, kept_pairs = route_slots(routes_g, order[0], counts[0])
     held = jnp.pad(
@@ -981,25 +1065,22 @@
     pads = ((0, 0), (0, SEQ_PAD - seq_len), (0, 0))
     rows = jnp.pad(images, pads).reshape(padded, width)
     back = jnp.pad(cotangent, pads).reshape(padded, width)
-    router = jnp.pad(w_router.T, ((0, 8 - SPECIALIST_TOTAL), (0, 0)))
     step = eight_step if lax.axis_size("dp") == 8 else plain_step
-    output, grad_images, grad_in, grad_out, dense = step(
-        rows, back, held_row, held_col, w_qkv, w_proj, router, w_in, w_out,
+    output, grad_images, grad_in, grad_out, grads, small = step(
+        rows, back, held_row, held_col, w_qkv.swapaxes(1, 2), w_proj, w_router.T, w_in, w_out,
         gain_one[None], gain_two[None],
     )
     cube = (img_count, SEQ_PAD, width)
-    dense = dense.astype(F32)
-    grads = dense[:, : 2 * local].reshape(4, local, width)
     return (
         output.reshape(cube)[:, :seq_len],
         grad_images.reshape(cube)[:, :seq_len],
-        grads[:3].transpose(0, 2, 1),
-        grads[3],
-        dense[0, 2 * local : 2 * local + SPECIALIST_TOTAL].T,
+        grads[:3].astype(F32).transpose(0, 2, 1),
+        grads[3].astype(F32),
+        small[0, :SPECIALIST_TOTAL].astype(F32).T,
         grad_in.astype(F32),
         grad_out.astype(F32),
-        dense[1, 2 * local],
-        dense[0, 2 * local + 8],
+        small[1, 0].astype(F32),
+        small[0, 8].astype(F32),
         kept_pairs.reshape(img_count, seq_len, TOPK),
     )
 

time: 269 us -> 236 us (0.88)
  Pallas kernels: 236 us -> 204 us
  other arithmetic: 10.8 us -> 17.9 us
  local copies, waits for them, and re-layouts: 16.5 us -> 11.3 us
  starting transfers between devices: 2.99 us -> 0 us
    pallas_call x1, Pallas kernels: 236 us -> 204 us  [eight_step(): pl.pallas_call(step_kernel, out_shape=tuple((jax.ShapeDtypeStruct(shape,...]
    ppermute x1 -> x0, starting transfers between devices: 2.99 us -> none  [eight_step(): held_pair = lax.ppermute(held_row, 'dp', [(i, i ^ 1) for i in range(n_dp)])]
  transfers between devices with their start and end apart: 1 -> 0, of which waited for: 0 -> 0; matrix products, arithmetic and copies ran while one was open for 2% -> 0% of each run, Pallas kernels for 0% -> 0%
where the time goes in v2:
time: 236 us
  Pallas kernels  204 us (86%)
  other arithmetic  17.9 us (8%)
  local copies, waits for them, and re-layouts  11.3 us (5%)
    pallas_call x1, Pallas kernels, eight_step(): pl.pallas_call(step_kernel, out_shape=tuple((jax.ShapeDtypeStruct(shape,...  204 us
    convert_element_type x1, other arithmetic, per_device(): grad_in.astype(F32)  7.05 us

profile of v2, /device:TPU:0, one launch (start us, length us, event | category | flops | bytes accessed | tf_op | source)
XLA Modules:
  0.0 235.8 jit_solution(18297131603594392536)
XLA Ops:
  1.3 0.7 copy.27
  2.0 0.1 eq.41
  2.2 0.1 eq.51
  2.3 0.1 fusion.12
  2.4 0.1 slice_reduce_fusion
  2.5 1.2 select_reduce_fusion
  3.7 0.8 multiply_reduce_fusion
  4.6 0.1 reshape.118
  4.7 0.2 copy.31
  5.0 0.0 copy-start.2
  5.0 0.0 copy-start.6
  5.0 0.0 copy-start.7
  5.0 0.0 copy-start.8
  5.0 0.8 copy.29.held
  5.9 0.0 copy-start.3
  5.9 2.8 %pad.12 = bf16[5,208,768]{2,1,0:T(8,128)(2,1)} pad(bf16[5,197,768]{2,1,0:T(8,128)(2,1)} %param.12, bf16[]{:T(256)} %constant.36.clone.1), padding=0_0x0_11x0_0 | pad | bytes 3110402 | tf_op jit(solution)/shard_map/jit(_pad)/pad | solution.py:1066
  8.6 0.0 copy-done.3
  8.6 1.3 pad.13
  9.9 0.0 copy-done.6
  9.9 0.0 copy-done.7
  9.9 0.0 copy-done.8
  10.0 1.3 concatenate.3.vectors
  11.2 0.0 copy-done.2
  11.2 204.2 %shard_map.195 = (bf16[1040,768]{1,0:T(8,128)(2,1)}, f32[1040,768]{1,0:T(8,128)}, bf16[4,768,768]{2,1,0:T(8,128)(2,1)}, bf16[4,768,768]{2,1,0:T(8,128)(2,1)}, bf...) custom-call(bf16[1040,768]{1,0:T(8,128)(2,1)} %bitcast.49, bf16[1040,768]{1,0:T(8,128)(2,1)} %bitcast.50, ...), custom_call_target="tpu_custom_call" | custom-call | flops 60000002048 | bytes 100000000 | tf_op jit(solution)/shard_map/pallas_call | solution.py:1024
  215.5 0.0 copy-start
  215.5 7.0 %convert_element_type.69 = f32[4,768,768]{2,1,0:T(8,128)} convert(bf16[4,768,768]{2,1,0:T(8,128)(2,1)} %get-tuple-element.20) | non-fusion elementwise | flops 2359296 | bytes 14155776 | tf_op jit(solution)/shard_map/convert_element_type | solution.py:1080
  222.5 0.0 copy-done
  222.5 0.0 copy-start.1
  222.5 4.6 %convert_element_type.70 = f32[4,768,768]{2,1,0:T(8,128)} convert(bf16[4,768,768]{2,1,0:T(8,128)(2,1)S(1)} %copy-done) | non-fusion elementwise | flops 2359296 | bytes 14155776 | tf_op jit(solution)/shard_map/convert_element_type | solution.py:1081
  227.1 0.0 copy-start.5
  227.1 0.0 copy-done.1
  227.1 0.0 copy-start.4
  227.1 1.9 slice.43
  229.0 0.0 copy-done.5
  229.0 1.3 convert_bitcast_fusion
  230.3 0.0 copy-done.4
  230.3 1.2 slice.42
  231.5 0.9 bitcast_convert_fusion
  232.4 1.3 convert_bitcast_fusion.1
  233.7 1.3 convert_reduce_fusion
  235.0 0.1 lt.53
  235.2 0.6 copy.30
  (18 shorter events, 0.2 us)
Async XLA Ops:
  5.0 6.3 %copy-start.2 = (s32[5,208,128]{2,1,0:T(8,128)}, s32[5,208,128]{2,1,0:T(8,128)S(1)}, u32[]{:S(2)}) copy-start(s32[5,208,128]{2,1,0:T(8,128)S(1)} %pad.14.clone) | copy-start | bytes 1597444
  5.0 4.9 %copy-start.6 = (bf16[768,4]{0,1:T(4,128)(2,1)S(1)}, bf16[768,4]{0,1:T(4,128)(2,1)}, u32[]{:S(2)}) copy-start(bf16[768,4]{0,1:T(4,128)(2,1)} %param.15) | copy-start | bytes 18436
  5.0 4.9 %copy-start.7 = (f32[768]{0:T(1024)S(1)}, f32[768]{0:T(1024)}, u32[]{:S(2)}) copy-start(f32[768]{0:T(1024)} %param.18) | copy-start | bytes 9220
  5.0 4.9 %copy-start.8 = (f32[768]{0:T(1024)S(1)}, f32[768]{0:T(1024)}, u32[]{:S(2)}) copy-start(f32[768]{0:T(1024)} %param.19) | copy-start | bytes 9220
  5.9 2.8 %copy-start.3 = (bf16[5,197,768]{2,1,0:T(8,128)(2,1)S(1)}, bf16[5,197,768]{2,1,0:T(8,128)(2,1)}, u32[]{:S(2)}) copy-start(bf16[5,197,768]{2,1,0:T(8,128)(2,1)} %param.23) | copy-start | bytes 4538884
  215.5 7.1 %copy-start = (bf16[4,768,768]{2,1,0:T(8,128)(2,1)S(1)}, bf16[4,768,768]{2,1,0:T(8,128)(2,1)}, u32[]{:S(2)}) copy-start(bf16[4,768,768]{2,1,0:T(8,128)(2,1)} %get-tuple-element.21) | copy-start | bytes 14155780
  222.5 4.6 %copy-start.1 = (f32[1040,768]{1,0:T(8,128)S(1)}, f32[1040,768]{1,0:T(8,128)}, u32[]{:S(2)}) copy-start(f32[1040,768]{1,0:T(8,128)} %get-tuple-element.17) | copy-start | bytes 9584644
  227.1 1.9 copy-start.5
  227.1 3.2 %copy-start.4 = (bf16[1040,768]{1,0:T(8,128)(2,1)S(1)}, bf16[1040,768]{1,0:T(8,128)(2,1)}, u32[]{:S(2)}) copy-start(bf16[1040,768]{1,0:T(8,128)(2,1)} %get-tuple-element.16) | copy-start | bytes 4792324

commit v3 on v2

--- a/solution.py
+++ b/solution.py
@@ -18,8 +18,10 @@
 PAIRED = SPECIALIST_TOTAL // 2
 LANES = 128
 PIECE = 128
+PER_TURN = 1
 RING = 6
 LAG = 2
+FORWARD = 4
 DENSE_CUTS = ((0, 96), (96, 96), (192, 96), (288, 96), (384, 16))
 DENSE_HALF = 400
 
@@ -29,7 +31,7 @@
 BF = jnp.bfloat16
 F32 = jnp.float32
 MESH = pl.DeviceIdType.MESH
-VMEM_LIMIT = 62 * 2**20
+VMEM_LIMIT = 63 * 2**20
 
 
 def dot(left, right, left_dim=1, right_dim=0):
@@ -393,7 +395,11 @@
 
 
 def plain_step(rows, back, held_row, held_col, w_qkv, w_proj, router, w_in, w_out, gain_one, gain_two):
-    padded, width = rows.shape
+    pads = ((0, 0), (0, SEQ_PAD - rows.shape[1]), (0, 0))
+    width = rows.shape[2]
+    rows, back = (jnp.pad(each, pads).reshape(-1, width) for each in (rows, back))
+    padded = rows.shape[0]
+    gain_one, gain_two = gain_one[None], gain_two[None]
     local = w_proj.shape[0]
     router = jnp.pad(router, ((0, 8 - SPECIALIST_TOTAL), (0, 0)))
     n_dp = lax.axis_size("dp")
@@ -454,8 +460,9 @@
 
 
 def step_kernel(
-    images, cotangent, held, held_col, w_qkv, w_proj, vectors, w_in, w_out,
+    held, held_col, w_qkv, w_proj, gain_first, gain_second, router_in, images_in, cotangent_in, w_in, w_out,
     output, grad_images, out_in, out_out, out_grads, out_small,
+    images, cotangent, stage, stage_sems, wide_router, gain_one, gain_two,
     held_pair, router, back_pair, tokens, tokens_pair, attended, partial, qkv, mixed,
     core_a, far_a, core_d, far_d, core_o, far_o, core_g, far_g, gate_part, gate_sum,
     gates, gates_pair, slots, inner, active, grads, sent, total, slot_in, slot_out,
@@ -484,7 +491,6 @@
     mine = pl.ds(pl.multiple_of(c * half, LANES), half)
     other = pl.ds(pl.multiple_of((1 - c) * half, LANES), half)
     local = w_proj.shape[0]
-    gain_one, gain_two = vectors.at[0:1], vectors.at[1:2]
     dense = active
     dense_landed, dense_middle = inner.at[:DENSE_HALF], inner.at[DENSE_HALF : 2 * DENSE_HALF]
 
@@ -503,13 +509,33 @@
             pltpu.make_async_copy(w_out.at[expert], slot_out.at[k % 2], weight_sems.at[1, k % 2]),
         ]
 
+    def fetch(k, i):
+        source = (cotangent_in, images_in)[k]
+        return pltpu.make_async_copy(source.at[i], stage.at[k, i % 2], stage_sems.at[k, i % 2])
+
+    for k in range(2):
+        for i in range(2):
+            fetch(k, i).start()
     for k in range(2):
         for copy in load(k):
             copy.start()
-    router[...] = vectors[8:16, :].astype(BF)
+    wide_router[...] = jnp.zeros_like(wide_router)
+    wide_router[:SPECIALIST_TOTAL, :] = router_in[...].astype(F32)
+    router[...] = wide_router[...].astype(BF)
+    gain_one[...] = gain_first[...][None]
+    gain_two[...] = gain_second[...][None]
     grad_dense[...] = jnp.zeros_like(grad_dense)
     grad_small[...] = jnp.zeros_like(grad_small)
     grad_last[...] = jnp.zeros_like(grad_last)
+
+    for i in range(count):
+        for k, target in enumerate((cotangent, images)):
+            fetch(k, i).wait()
+            rows = stage[k, i % 2].astype(F32)
+            rows = jnp.concatenate([rows, jnp.zeros((SEQ_PAD - SEQ, width), F32)])
+            target[image_rows(i), :] = rows.astype(BF)
+            if i + 2 < count:
+                fetch(k, i + 2).start()
 
     @pl.when(inside)
     def _():
@@ -721,7 +747,16 @@
 
     last = pieces + len(DENSE_CUTS)
 
+    main_turns = pieces // PER_TURN
+
     def tick(n):
+        if isinstance(n, int) and n >= main_turns:
+            turn_piece(pieces + n - main_turns)
+        else:
+            for j in range(PER_TURN):
+                turn_piece(n * PER_TURN + j)
+
+    def turn_piece(n):
         def when(n, body):
             if isinstance(n, int):
                 if 0 <= n < last:
@@ -753,7 +788,7 @@
 
         @pl.when(outside)
         def _():
-            when(n - 2 * LAG, forward)
+            when(n - FORWARD, forward)
 
     def lift(n):
         @pl.when(outside)
@@ -939,7 +974,7 @@
         dense_copy(i).start()
     join_core(bee, count - 1, partial, core_a, far_a)
     loop(count, lambda i: join_core(oh, i, moe_part, core_o, far_o))
-    while turn < pieces:
+    while turn < main_turns:
         tick(turn)
         turn += 1
     for i in range(count - 2, count):
@@ -957,7 +992,7 @@
         if i:
             emit(i - 1)
     emit(count - 1)
-    while turn < last + 2 * LAG:
+    while turn + pieces - main_turns < last + max(LAG, FORWARD):
         tick(turn)
         turn += 1
 
@@ -995,12 +1030,10 @@
 
 
 def eight_step(rows, back, held_row, held_col, w_qkv, w_proj, router, w_in, w_out, gain_one, gain_two):
-    padded, width = rows.shape
+    count, seq_len, width = rows.shape
+    padded = count * SEQ_PAD
     local = w_proj.shape[0]
-    count = padded // SEQ_PAD
     half = width // 2
-    gap = jnp.zeros((6, width), F32)
-    vectors = jnp.concatenate([gain_one, gain_two, gap, router.astype(F32), gap[:4]])
     wide = 2 * width + LANES
     pieces = 4 * width // PIECE
     last = pieces + len(DENSE_CUTS)
@@ -1010,6 +1043,8 @@
     part = ((padded, half), BF)
     thin = ((padded, LANES), BF)
     square = (width, width)
+    start = [flat, flat, ((2, 2, seq_len, width), BF)]
+    early = [((8, width), F32), ((1, width), F32), ((1, width), F32)]
     scratch = [((8, padded), jnp.int32), ((8, width), BF)] + [flat] * 5 + [((3, padded, local), BF), ((padded, local), BF)]
     scratch += [part] * 6 + [thin] * 4
     scratch += [((8, padded), F32)] * 2 + [((2 * CAP_PAD, width), BF)] * 4
@@ -1024,16 +1059,86 @@
     return pl.pallas_call(
         step_kernel,
         out_shape=tuple(jax.ShapeDtypeStruct(shape, kind) for shape, kind in outs),
-        in_specs=[vmem] * 7 + [hbm] * 2,
+        in_specs=[vmem] * 7 + [hbm] * 4,
         out_specs=tuple(hbm for _ in outs),
-        scratch_shapes=[pltpu.VMEM(shape, kind) for shape, kind in scratch] + sems,
+        scratch_shapes=[pltpu.VMEM(*each) for each in start]
+        + [dma((2, 2))]
+        + [pltpu.VMEM(*each) for each in early + scratch]
+        + sems,
         compiler_params=pltpu.CompilerParams(
             collective_id=0, has_side_effects=True, vmem_limit_bytes=VMEM_LIMIT
         ),
         cost_estimate=pl.CostEstimate(flops=6 * 10**10, bytes_accessed=10**8, transcendentals=0),
     )(
-        rows, back, held_row, held_col, w_qkv, w_proj, vectors, w_in, w_out
-    )
+        held_row, held_col, w_qkv, w_proj, gain_one, gain_two, router, rows, back, w_in, w_out
+    )
+
+
+def trim_kernel(
+    images_count, output, grad_images, grad_in, grad_out, grads, small,
+    output_to, images_to, in_to, out_to, qkv_to, proj_to, router_to, first_to, second_to,
+):
+    turn = pl.program_id(0)
+    in_to[...] = grad_in[...].astype(F32)
+    out_to[...] = grad_out[...].astype(F32)
+
+    @pl.when(turn < images_count)
+    def _():
+        output_to[0] = output[0][:SEQ]
+        images_to[0] = grad_images[0][:SEQ]
+
+    @pl.when(turn < 4)
+    def _():
+        rows = grads[0].astype(F32)
+
+        @pl.when(turn < 3)
+        def _():
+            qkv_to[0] = rows
+
+        @pl.when(turn == 3)
+        def _():
+            proj_to[...] = rows
+
+    @pl.when(turn == 0)
+    def _():
+        rows = small[...].astype(F32)
+        router_to[...] = rows[0, :SPECIALIST_TOTAL]
+        second_to[...] = rows[0, 8]
+        first_to[...] = rows[1, 0]
+
+
+def trim(output, grad_images, grad_in, grad_out, grads, small):
+    experts, width, _ = grad_in.shape
+    local = grads.shape[1]
+    images = output.shape[0]
+    turns = 12
+    rows = experts * width // turns
+    cube = lambda size, count: pl.BlockSpec(
+        (1, size, width), lambda i: (jnp.minimum(i, count - 1), 0, 0)
+    )
+    tall = pl.BlockSpec((rows, width), lambda i: (i, 0))
+    whole = lambda *shape: pl.BlockSpec(shape, lambda i: (0,) * len(shape))
+    flat = (experts * width, width)
+    shapes = [(output.shape[0], SEQ, width), (output.shape[0], SEQ, width), flat, flat]
+    shapes += [(3, local, width), (local, width), (experts, width), (width,), (width,)]
+    kinds = [BF] + [F32] * 8
+    got = pl.pallas_call(
+        functools.partial(trim_kernel, images),
+        grid=(turns,),
+        out_shape=tuple(jax.ShapeDtypeStruct(a, b) for a, b in zip(shapes, kinds)),
+        in_specs=[
+            cube(SEQ_PAD, images), cube(SEQ_PAD, images), tall, tall, cube(local, 4),
+            whole(*small.shape),
+        ],
+        out_specs=(
+            cube(SEQ, images), cube(SEQ, images), tall, tall, cube(local, 3),
+            whole(local, width), whole(experts, width), whole(width), whole(width),
+        ),
+        compiler_params=pltpu.CompilerParams(vmem_limit_bytes=VMEM_LIMIT),
+        cost_estimate=pl.CostEstimate(flops=0, bytes_accessed=4 * 10**7, transcendentals=0),
+    )(output, grad_images, grad_in.reshape(flat), grad_out.reshape(flat), grads, small)
+    shape = (experts, width, width)
+    return (*got[:2], got[2].reshape(shape), got[3].reshape(shape), *got[4:])
 
 
 def per_device(
@@ -1062,25 +1167,25 @@
     padded = img_count * SEQ_PAD
     held_col = held.reshape(padded, LANES)
     held_row = held_col[:, :8].T
-    pads = ((0, 0), (0, SEQ_PAD - seq_len), (0, 0))
-    rows = jnp.pad(images, pads).reshape(padded, width)
-    back = jnp.pad(cotangent, pads).reshape(padded, width)
     step = eight_step if lax.axis_size("dp") == 8 else plain_step
     output, grad_images, grad_in, grad_out, grads, small = step(
-        rows, back, held_row, held_col, w_qkv.swapaxes(1, 2), w_proj, w_router.T, w_in, w_out,
-        gain_one[None], gain_two[None],
+        images, cotangent, held_row, held_col, w_qkv.swapaxes(1, 2), w_proj, w_router.T, w_in, w_out,
+        gain_one, gain_two,
     )
     cube = (img_count, SEQ_PAD, width)
+    output, grad_images, grad_in, grad_out, grad_qkv, grad_proj, grad_router, first, second = trim(
+        output.reshape(cube), grad_images.reshape(cube), grad_in, grad_out, grads, small
+    )
     return (
-        output.reshape(cube)[:, :seq_len],
-        grad_images.reshape(cube)[:, :seq_len],
-        grads[:3].astype(F32).transpose(0, 2, 1),
-        grads[3].astype(F32),
-        small[0, :SPECIALIST_TOTAL].astype(F32).T,
-        grad_in.astype(F32),
-        grad_out.astype(F32),
-        small[1, 0].astype(F32),
-        small[0, 8].astype(F32),
+        output,
+        grad_images,
+        grad_qkv.transpose(0, 2, 1),
+        grad_proj,
+        grad_router.T,
+        grad_in,
+        grad_out,
+        first,
+        second,
         kept_pairs.reshape(img_count, seq_len, TOPK),
     )
 

time: 236 us -> 229 us (0.970)
  Pallas kernels: 204 us -> 222 us
  other arithmetic: 17.9 us -> 1.48 us
  local copies, waits for them, and re-layouts: 11.3 us -> 2.83 us
    pallas_call x0 -> x1, Pallas kernels: none -> 16.2 us  [trim(): pl.pallas_call(functools.partial(trim_kernel, images), grid=(turns,), out...]
    convert_element_type x5 -> x0, other arithmetic: 13.8 us -> none  [the longest x1 7.05 us: per_device(): grad_in.astype(F32)]
    pad x2 -> x0, local copies, waits for them, and re-layouts: 4.02 us -> none  [the longest x1 2.76 us: per_device(): rows = jnp.pad(images, pads).reshape(padded, width)]
    slice x3 -> x0, local copies, waits for them, and re-layouts: 3.1 us -> none  [the longest x1 1.87 us: per_device(): grad_images.reshape(cube)[:, :seq_len]]
    transpose x2 -> x0, other arithmetic: 2.66 us -> none  [the longest x1 1.35 us: per_device(): grads[:3].astype(F32).transpose(0, 2, 1)]
where the time goes in v3:
time: 229 us
  Pallas kernels  222 us (97%)
  local copies, waits for them, and re-layouts  2.83 us (1%)
    pallas_call x1, Pallas kernels, eight_step(): pl.pallas_call(step_kernel, out_shape=tuple((jax.ShapeDtypeStruct(shape,...  206 us
    pallas_call x1, Pallas kernels, trim(): pl.pallas_call(functools.partial(trim_kernel, images), grid=(turns,), out...  16.2 us

profile of v3, /device:TPU:0, one launch (start us, length us, event | category | flops | bytes accessed | tf_op | source)
XLA Modules:
  0.0 228.8 jit_solution(3146177544565884633)
XLA Ops:
  1.3 0.7 copy.27
  2.0 0.1 eq.41
  2.2 0.1 eq.51
  2.3 0.1 fusion.12
  2.4 0.1 slice_reduce_fusion
  2.5 1.2 select_reduce_fusion
  3.7 0.8 multiply_reduce_fusion
  4.6 0.1 reshape.114
  4.7 0.2 copy.31
  5.0 0.0 copy-start
  5.0 0.8 copy.29.held
  5.8 0.0 copy-done
  5.8 206.1 %shard_map.195 = (bf16[1040,768]{1,0:T(8,128)(2,1)}, f32[1040,768]{1,0:T(8,128)}, bf16[4,768,768]{2,1,0:T(8,128)(2,1)}, bf16[4,768,768]{2,1,0:T(8,128)(2,1)}, bf...) custom-call(s32[8,1040]{1,0:T(8,128)} %copy.29.held, s32[1040,128]{1,0:T(8,128)} %bitcast.43, ...), custom_call_target="tpu_custom_call" | custom-call | flops 60000002048 | bytes 100000000 | tf_op jit(solution)/shard_map/pallas_call | solution.py:1059
  211.9 16.2 %shard_map.196 = (bf16[5,197,768]{2,1,0:T(8,128)(2,1)}, f32[5,197,768]{2,1,0:T(8,128)}, f32[3072,768]{1,0:T(8,128)}, f32[3072,768]{1,0:T(8,128)}, f32[3,192,768]...) custom-call(bf16[5,208,768]{2,1,0:T(8,128)(2,1)} %bitcast.44, ...), custom_call_target="tpu_custom_call" | custom-call | bytes 40000000 | tf_op jit(solution)/shard_map/pallas_call | solution.py:1125
  228.1 0.1 lt.53
  228.2 0.6 copy.30
  (13 shorter events, 0.2 us)
Async XLA Ops:
  5.0 0.9 copy-start

commit v4 on v3

--- a/solution.py
+++ b/solution.py
@@ -158,7 +158,9 @@
     return rows * half, slope
 
 
-def expert_rows(expert, tokens, back, held, gates, w_in, w_out, factors, offset, sent, tick):
+def expert_rows(
+    expert, tokens, back, held, gates, w_in, w_out, factors, offset, sent, tick, ahead=False
+):
     width = tokens.shape[1]
     row = held[pl.ds(expert, 1), :]
     gate = gates[pl.ds(expert, 1), :]
@@ -169,7 +171,11 @@
         pick = jnp.where(hit, 1.0, 0.0).astype(BF)
         scale = jnp.sum(jnp.where(hit, gate, 0.0), axis=1, keepdims=True)
         buffer = dot(pick, tokens[...]).astype(BF)
-        raw = dot(pick, back[...])
+        if ahead:
+            at = pl.ds(pl.multiple_of(offset + i * TILE, 16), TILE)
+            raw = factors[3][at, :].astype(F32)
+        else:
+            raw = dot(pick, back[...])
         grad = (scale * raw).astype(BF)
         value, slope = gelu_both(dot(buffer, w_in[...]))
         value = value.astype(BF)
@@ -188,6 +194,19 @@
             sent[at, 2 * width :] = jnp.where(lane, share, 0.0).astype(BF)
         if tick is not None:
             tick(i)
+        return carry
+
+    lax.fori_loop(0, CAP_PAD // TILE, tile, 0)
+
+
+def raw_rows(expert, back, held, grads, offset):
+    row = held[pl.ds(expert, 1), :]
+
+    def tile(i, carry):
+        ids = lax.broadcasted_iota(jnp.int32, (TILE, row.shape[1]), 0) + i * TILE
+        pick = jnp.where(ids == row, 1.0, 0.0).astype(BF)
+        at = pl.ds(pl.multiple_of(offset + i * TILE, 16), TILE)
+        grads[at, :] = dot(pick, back[...]).astype(BF)
         return carry
 
     lax.fori_loop(0, CAP_PAD // TILE, tile, 0)
@@ -536,6 +555,7 @@
             target[image_rows(i), :] = rows.astype(BF)
             if i + 2 < count:
                 fetch(k, i + 2).start()
+    attention_image(0, images, w_qkv, w_proj, gain_one, partial, qkv, mixed)
 
     @pl.when(inside)
     def _():
@@ -660,7 +680,10 @@
 
     def attention_step(step):
         def first(i):
-            attention_image(i, images, w_qkv, w_proj, gain_one, partial, qkv, mixed)
+            @pl.when(i > 0)
+            def _():
+                attention_image(i, images, w_qkv, w_proj, gain_one, partial, qkv, mixed)
+
             rs_copy(ATT_RS, i, partial, core_a).start()
 
         def norm(i):
@@ -756,10 +779,10 @@
             for j in range(PER_TURN):
                 turn_piece(n * PER_TURN + j)
 
-    def turn_piece(n):
+    def turn_piece(n, start=0, stop=last):
         def when(n, body):
             if isinstance(n, int):
-                if 0 <= n < last:
+                if start <= n < stop:
                     body(n)
             else:
                 pl.when(n >= 0)(functools.partial(body, n))
@@ -823,25 +846,32 @@
             copy.wait()
         kept = factors if k < PAIRED else None
         base = turn
+
+        def give(i):
+            token_copy(i).wait_recv()
+            token_give(i).start()
+
+        def give_first(i):
+            @pl.when(i == 0)
+            def _():
+                loop(count - 2, give)
+
         expert_rows(
             expert, tokens, cotangent, held, gates, *weights, kept, 0, sent,
-            (lambda i, base=base: tick(base + i)) if k else None,
+            (lambda i, base=base: tick(base + i)) if k else give_first,
         )
         if k:
             turn += 2
         ends = k == SPECIALIST_TOTAL - 1
         if k == 0:
-
-            def give(i):
-                token_copy(i).wait_recv()
-                token_give(i).start()
-
-            loop(count, give)
+            for i in range(count - 2, count):
+                give(i)
             loop(count, cot_land)
             return_rows(expert, held_col, sent, total, True, None, None, 0, 2)
-            loop(count, lambda i: token_give(i).wait_recv())
             loop(count, cot_end)
             held_copy.wait()
+            raw_rows(expert, back_pair, held_pair, grads, CAP_PAD)
+            loop(count, lambda i: token_give(i).wait_recv())
             gates_pair[...] = softmax_of(dot(router[...], tokens_pair[...], 1, 1), 0)
         else:
             return_rows(
@@ -854,7 +884,7 @@
             base = turn
             expert_rows(
                 expert, tokens_pair, back_pair, held_pair, gates_pair, *weights, kept, CAP_PAD, None,
-                (lambda i, base=base: tick(base + i)) if k else None,
+                (lambda i, base=base: tick(base + i)) if k else None, k == 0,
             )
             if k:
                 turn += 2
@@ -870,9 +900,10 @@
 
                 weight_rows(left, right, main, (2 * k + kind) * width, after)
             if k == 0:
-                return_rows(expert, held_col, sent, total, True, None, None, 2)
+                return_rows(expert, held_col, sent, total, True, None, None, 2, 4)
                 tick(turn)
                 turn += 1
+                return_rows(expert, held_col, sent, total, True, None, None, 4)
         if k == PAIRED - 1:
 
             def tokens_sent(i):
@@ -977,24 +1008,32 @@
     while turn < main_turns:
         tick(turn)
         turn += 1
-    for i in range(count - 2, count):
-        join_far(bee, i, partial, far_a, sums)
-        finish(i - 1)
+
+    def drain(n):
+        turn_piece(pieces + n, 0, pieces)
+
+    drain(0)
+    join_far(bee, count - 2, partial, far_a, sums)
+    finish(count - 3)
+    drain(1)
+    join_far(bee, count - 1, partial, far_a, sums)
+    finish(count - 2)
     finish(count - 1)
     for side, rows in enumerate((grad_small, grad_last)):
         dense[dense_view(small, side), :] = rows[...].astype(BF)
     dense_copy(small).start()
+    for n in range(2, FORWARD):
+        drain(n)
     for i in range(len(DENSE_CUTS)):
         dense_join(i)
-        tick(turn)
-        turn += 1
+        turn_piece(pieces + i, pieces)
+    for n in range(len(DENSE_CUTS), len(DENSE_CUTS) + FORWARD):
+        turn_piece(pieces + n, pieces)
+    for i in range(count):
         join_far(oh, i, moe_part, far_o, moe)
         if i:
             emit(i - 1)
     emit(count - 1)
-    while turn + pieces - main_turns < last + max(LAG, FORWARD):
-        tick(turn)
-        turn += 1
 
     def rest(i):
         rs_copy(D_RS, i, sum_part, core_d).wait_send()
@@ -1111,7 +1150,7 @@
     experts, width, _ = grad_in.shape
     local = grads.shape[1]
     images = output.shape[0]
-    turns = 12
+    turns = 8
     rows = experts * width // turns
     cube = lambda size, count: pl.BlockSpec(
         (1, size, width), lambda i: (jnp.minimum(i, count - 1), 0, 0)

time: 229 us -> 229 us (level)
  no operation moved by 1% of the time
where the time goes in v4:
time: 229 us
  Pallas kernels  222 us (97%)
  local copies, waits for them, and re-layouts  2.83 us (1%)
    pallas_call x1, Pallas kernels, eight_step(): pl.pallas_call(step_kernel, out_shape=tuple((jax.ShapeDtypeStruct(shape,...  207 us
    pallas_call x1, Pallas kernels, trim(): pl.pallas_call(functools.partial(trim_kernel, images), grid=(turns,), out...  15.7 us

profile of v4, /device:TPU:0, one launch (start us, length us, event | category | flops | bytes accessed | tf_op | source)
XLA Modules:
  0.0 228.8 jit_solution(2825007803987938910)
XLA Ops:
  1.3 0.7 copy.27
  2.0 0.1 eq.41
  2.2 0.1 eq.51
  2.3 0.1 fusion.12
  2.4 0.1 slice_reduce_fusion
  2.5 1.2 select_reduce_fusion
  3.7 0.8 multiply_reduce_fusion
  4.6 0.1 reshape.114
  4.7 0.2 copy.31
  5.0 0.0 copy-start
  5.0 0.8 copy.29.held
  5.8 0.0 copy-done
  5.8 206.6 %shard_map.195 = (bf16[1040,768]{1,0:T(8,128)(2,1)}, f32[1040,768]{1,0:T(8,128)}, bf16[4,768,768]{2,1,0:T(8,128)(2,1)}, bf16[4,768,768]{2,1,0:T(8,128)(2,1)}, bf...) custom-call(s32[8,1040]{1,0:T(8,128)} %copy.29.held, s32[1040,128]{1,0:T(8,128)} %bitcast.43, ...), custom_call_target="tpu_custom_call" | custom-call | flops 60000002048 | bytes 100000000 | tf_op jit(solution)/shard_map/pallas_call | solution.py:1098
  212.4 15.7 %shard_map.196 = (bf16[5,197,768]{2,1,0:T(8,128)(2,1)}, f32[5,197,768]{2,1,0:T(8,128)}, f32[3072,768]{1,0:T(8,128)}, f32[3072,768]{1,0:T(8,128)}, f32[3,192,768]...) custom-call(bf16[5,208,768]{2,1,0:T(8,128)(2,1)} %bitcast.44, ...), custom_call_target="tpu_custom_call" | custom-call | bytes 40000000 | tf_op jit(solution)/shard_map/pallas_call | solution.py:1164
  228.1 0.1 lt.53
  228.2 0.6 copy.30
  (13 shorter events, 0.2 us)
Async XLA Ops:
  5.0 0.9 copy-start

commit v5 on v3

--- a/solution.py
+++ b/solution.py
@@ -1111,7 +1111,7 @@
     experts, width, _ = grad_in.shape
     local = grads.shape[1]
     images = output.shape[0]
-    turns = 12
+    turns = 8
     rows = experts * width // turns
     cube = lambda size, count: pl.BlockSpec(
         (1, size, width), lambda i: (jnp.minimum(i, count - 1), 0, 0)

time: 229 us -> 229 us (level)
  no operation moved by 1% of the time
where the time goes in v5:
time: 229 us; the launch traced here: 228 us
  Pallas kernels  222 us (97%)
  local copies, waits for them, and re-layouts  2.83 us (1%)
    pallas_call x1, Pallas kernels, eight_step(): pl.pallas_call(step_kernel, out_shape=tuple((jax.ShapeDtypeStruct(shape,...  206 us
    pallas_call x1, Pallas kernels, trim(): pl.pallas_call(functools.partial(trim_kernel, images), grid=(turns,), out...  15.7 us

profile of v5, /device:TPU:0, one launch (start us, length us, event | category | flops | bytes accessed | tf_op | source)
XLA Modules:
  0.0 228.4 jit_solution(4096335438308484851)
XLA Ops:
  1.3 0.7 copy.27
  2.0 0.1 eq.41
  2.2 0.1 eq.51
  2.3 0.1 fusion.12
  2.4 0.1 slice_reduce_fusion
  2.5 1.2 select_reduce_fusion
  3.7 0.8 multiply_reduce_fusion
  4.6 0.1 reshape.114
  4.7 0.2 copy.31
  5.0 0.0 copy-start
  5.0 0.8 copy.29.held
  5.8 0.0 copy-done
  5.8 206.1 %shard_map.195 = (bf16[1040,768]{1,0:T(8,128)(2,1)}, f32[1040,768]{1,0:T(8,128)}, bf16[4,768,768]{2,1,0:T(8,128)(2,1)}, bf16[4,768,768]{2,1,0:T(8,128)(2,1)}, bf...) custom-call(s32[8,1040]{1,0:T(8,128)} %copy.29.held, s32[1040,128]{1,0:T(8,128)} %bitcast.43, ...), custom_call_target="tpu_custom_call" | custom-call | flops 60000002048 | bytes 100000000 | tf_op jit(solution)/shard_map/pallas_call | solution.py:1059
  211.9 15.7 %shard_map.196 = (bf16[5,197,768]{2,1,0:T(8,128)(2,1)}, f32[5,197,768]{2,1,0:T(8,128)}, f32[3072,768]{1,0:T(8,128)}, f32[3072,768]{1,0:T(8,128)}, f32[3,192,768]...) custom-call(bf16[5,208,768]{2,1,0:T(8,128)(2,1)} %bitcast.44, ...), custom_call_target="tpu_custom_call" | custom-call | bytes 40000000 | tf_op jit(solution)/shard_map/pallas_call | solution.py:1125
  227.6 0.1 lt.53
  227.8 0.6 copy.30
  (13 shorter events, 0.2 us)
Async XLA Ops:
  5.0 0.9 copy-start
